TPU v7x, 512 devices: a whole 4x8x8 slice. The times are simulated.
512 devices in a mesh: site: 16 (over z, core), sector: 32 (over y, x).
Axes of the slice: x: 4, y: 8, z: 8, core: 2. Of those that a mesh axis runs over, the one named last changes fastest.
Arguments:
- left_env: bfloat16 [32, 128, 128], P('sector'), may hold values from -4 to 4
- mps_bra: bfloat16 [16, 512, 128, 128], P('site', 'sector'), may hold values from -0.5 to 0.5
- mps_ket: bfloat16 [16, 512, 128, 128], P('site', 'sector'), may hold values from -0.5 to 0.5
- joining_out: int32 [16, 512, 1], P('site', 'sector'), may hold values from 0 to 31; in each aligned block of 16 rows (0 to 15, 16 to 31, ..., all dimensions but the last counted through in order) at most 2 rows name the same one
- joining_mpo: int32 [16, 512], P('site', 'sector'), may hold values from 0 to 7
- owner: int32 [32], replicated, may hold values from 0 to 31, each once
- mpo_weight: float32 [16, 8], P('site'), may hold values from -1.5 to 1.5
Outputs:
- envs: bfloat16 [16, 32, 128, 128], P('site', 'sector')
Inputs may be any that keep to these rules, and one draw needn't show every extreme that they name: `joining_out`: at each site, among the 16 triples of one input slot at most 2 name the same output slot.
All inputs are finite; a program needn't handle non-finite values.
Results may differ from a plain program's by a relative error of at most 0.04.
Values may be sent and summed in bfloat16 or wider, within the bound.
A program may use at most 64 MiB of HBM per device.

v0:
```python
import jax
import jax.numpy as jnp
from jax import lax
from jax.sharding import PartitionSpec as P


def from_behind(x, axis, by):
    count = lax.axis_size(axis)
    pairs = [(i, i + by) for i in range(count) if 0 <= i + by < count]
    return lax.ppermute(x, axis, pairs)


def lookups(joining_out, joining_mpo, owner, mpo_weight):
    sectors = owner.shape[0]
    terms = mpo_weight.shape[1]
    outputs = joining_out[0, :, 0]
    target = jnp.sum(
        jnp.where(
            outputs[:, None] == jnp.arange(sectors, dtype=jnp.int32)[None, :], owner[None, :], 0
        ),
        axis=1,
    )
    weights = jnp.sum(
        jnp.where(
            joining_mpo[0][:, None] == jnp.arange(terms, dtype=jnp.int32)[None, :],
            mpo_weight[0][None, :],
            0.0,
        ),
        axis=1,
    )
    return (target, weights)


def local(left_env, mps_bra, mps_ket, joining_out, joining_mpo, owner, mpo_weight):
    site_index = lax.axis_index("site")
    slots = lax.axis_size("sector")
    target, weights = lookups(joining_out, joining_mpo, owner, mpo_weight)
    hits = (target[:, None] == jnp.arange(slots, dtype=jnp.int32)[None, :]).astype(jnp.float32)
    routing = hits * weights[:, None]
    start_env = jnp.where(site_index == 0, left_env, jnp.zeros_like(left_env))

    def triple_sums(current):
        inner_part = jnp.einsum(
            "ab,kbc->kac", current[0], mps_ket[0], preferred_element_type=jnp.float32
        ).astype(jnp.bfloat16)
        product = jnp.einsum(
            "kai,kac->kic", mps_bra[0], inner_part, preferred_element_type=jnp.float32
        )
        return jnp.einsum("kn,kic->nic", routing, product).astype(jnp.bfloat16)

    def section(step_index, current):
        partial_value = triple_sums(current)
        received = lax.all_to_all(partial_value, "sector", split_axis=0, concat_axis=0, tiled=True)
        fresh = jnp.sum(received.astype(jnp.float32), axis=0, keepdims=True).astype(jnp.bfloat16)
        passed = from_behind(fresh, "site", 1)
        return jnp.where(site_index == step_index + 1, passed, current)

    final_env = lax.fori_loop(0, lax.axis_size("site") - 1, section, start_env)
    return final_env[None]


def solution(mesh):
    return jax.shard_map(
        local,
        mesh=mesh,
        in_specs=(
            P("sector", None, None),
            P("site", "sector", None, None),
            P("site", "sector", None, None),
            P("site", "sector", None),
            P("site", "sector"),
            P(),
            P("site", None),
        ),
        out_specs=P("site", "sector", None, None),
        check_vma=False,
    )
```

profile of v0, /device:TPU:1, one launch (start us, length us, event | category | flops | bytes accessed | tf_op | source)
XLA Modules:
  0.0 606.1 jit_solution(12428045117503721897)
XLA Ops:
  0.0 1.4 copy.11
  2.3 0.6 copy-done.4
  3.0 602.5 %while.14 = (s32[]{:T(128)}, bf16[1,128,128]{2,1,0:T(8,128)(2,1)S(1)}, s32[]{:T(128)}, bf16[1,16,128,128]{2,3,1,0:T(8,128)(2,1)S(1)}, bf16[1,16,128,128]{3,2,1,0...) while((s32[]{:T(128)}, ...), condition=%wide.region_4.5_spmd.clone, body=%wide.region_2.4_spmd.clone.sunk | while | flops 151782400 | bytes 9732337 | solution.py:58
  5.0 35.9 %all_to_all.11 = bf16[32,128,128]{2,1,0:T(8,128)(2,1)S(1)} all-to-all(bf16[32,128,128]{2,1,0:T(8,128)(2,1)S(1)} %copy.15), channel_id=1, replica_groups=mesh['site'=16,'sector'=32] {'sector'}, dimensions={0} | all-to-all | bytes 2097152 | tf_op jit(solution)/shard_map/while/body/eval_jaxpr/all_to_all | solution.py:53
  41.1 7.3 %collective-permute-start = (bf16[1,128,128]{2,1,0:T(8,128)(2,1)S(1)}, bf16[1,128,128]{2,1,0:T(8,128)(2,1)S(1)}, u32[]{:S(2)}, u32[]{:S(2)}) collective-permute-start(bf16[1,128,128]{2,1,0:T(8,128)(2,1)S(1)} %bitcast.41), channel_id=1, source_target_pairs={{0,32},{32,64},{64,96},{96,128},{128,160},{160,192},{192,224},{224... | collective-permute-start | bytes 98312 | tf_op jit(solution)/shard_map/while/body/eval_jaxpr/ppermute | solution.py:10
  48.4 1.0 collective-permute-done
  51.3 31.4 %all_to_all.11 = bf16[32,128,128]{2,1,0:T(8,128)(2,1)S(1)} all-to-all(bf16[32,128,128]{2,1,0:T(8,128)(2,1)S(1)} %copy.15), channel_id=1, replica_groups=mesh['site'=16,'sector'=32] {'sector'}, dimensions={0} | all-to-all | bytes 2097152 | tf_op jit(solution)/shard_map/while/body/eval_jaxpr/all_to_all | solution.py:53
  82.8 6.6 %collective-permute-start = (bf16[1,128,128]{2,1,0:T(8,128)(2,1)S(1)}, bf16[1,128,128]{2,1,0:T(8,128)(2,1)S(1)}, u32[]{:S(2)}, u32[]{:S(2)}) collective-permute-start(bf16[1,128,128]{2,1,0:T(8,128)(2,1)S(1)} %bitcast.41), channel_id=1, source_target_pairs={{0,32},{32,64},{64,96},{96,128},{128,160},{160,192},{192,224},{224... | collective-permute-start | bytes 98312 | tf_op jit(solution)/shard_map/while/body/eval_jaxpr/ppermute | solution.py:10
  89.5 1.0 collective-permute-done
  92.4 29.9 %all_to_all.11 = bf16[32,128,128]{2,1,0:T(8,128)(2,1)S(1)} all-to-all(bf16[32,128,128]{2,1,0:T(8,128)(2,1)S(1)} %copy.15), channel_id=1, replica_groups=mesh['site'=16,'sector'=32] {'sector'}, dimensions={0} | all-to-all | bytes 2097152 | tf_op jit(solution)/shard_map/while/body/eval_jaxpr/all_to_all | solution.py:53
  122.5 8.1 %collective-permute-start = (bf16[1,128,128]{2,1,0:T(8,128)(2,1)S(1)}, bf16[1,128,128]{2,1,0:T(8,128)(2,1)S(1)}, u32[]{:S(2)}, u32[]{:S(2)}) collective-permute-start(bf16[1,128,128]{2,1,0:T(8,128)(2,1)S(1)} %bitcast.41), channel_id=1, source_target_pairs={{0,32},{32,64},{64,96},{96,128},{128,160},{160,192},{192,224},{224... | collective-permute-start | bytes 98312 | tf_op jit(solution)/shard_map/while/body/eval_jaxpr/ppermute | solution.py:10
  130.6 1.0 collective-permute-done
  133.5 28.3 %all_to_all.11 = bf16[32,128,128]{2,1,0:T(8,128)(2,1)S(1)} all-to-all(bf16[32,128,128]{2,1,0:T(8,128)(2,1)S(1)} %copy.15), channel_id=1, replica_groups=mesh['site'=16,'sector'=32] {'sector'}, dimensions={0} | all-to-all | bytes 2097152 | tf_op jit(solution)/shard_map/while/body/eval_jaxpr/all_to_all | solution.py:53
  162.0 10.1 %collective-permute-start = (bf16[1,128,128]{2,1,0:T(8,128)(2,1)S(1)}, bf16[1,128,128]{2,1,0:T(8,128)(2,1)S(1)}, u32[]{:S(2)}, u32[]{:S(2)}) collective-permute-start(bf16[1,128,128]{2,1,0:T(8,128)(2,1)S(1)} %bitcast.41), channel_id=1, source_target_pairs={{0,32},{32,64},{64,96},{96,128},{128,160},{160,192},{192,224},{224... | collective-permute-start | bytes 98312 | tf_op jit(solution)/shard_map/while/body/eval_jaxpr/ppermute | solution.py:10
  172.2 1.0 collective-permute-done
  175.2 26.2 %all_to_all.11 = bf16[32,128,128]{2,1,0:T(8,128)(2,1)S(1)} all-to-all(bf16[32,128,128]{2,1,0:T(8,128)(2,1)S(1)} %copy.15), channel_id=1, replica_groups=mesh['site'=16,'sector'=32] {'sector'}, dimensions={0} | all-to-all | bytes 2097152 | tf_op jit(solution)/shard_map/while/body/eval_jaxpr/all_to_all | solution.py:53
  201.5 11.6 %collective-permute-start = (bf16[1,128,128]{2,1,0:T(8,128)(2,1)S(1)}, bf16[1,128,128]{2,1,0:T(8,128)(2,1)S(1)}, u32[]{:S(2)}, u32[]{:S(2)}) collective-permute-start(bf16[1,128,128]{2,1,0:T(8,128)(2,1)S(1)} %bitcast.41), channel_id=1, source_target_pairs={{0,32},{32,64},{64,96},{96,128},{128,160},{160,192},{192,224},{224... | collective-permute-start | bytes 98312 | tf_op jit(solution)/shard_map/while/body/eval_jaxpr/ppermute | solution.py:10
  213.1 1.0 collective-permute-done
  216.1 24.9 %all_to_all.11 = bf16[32,128,128]{2,1,0:T(8,128)(2,1)S(1)} all-to-all(bf16[32,128,128]{2,1,0:T(8,128)(2,1)S(1)} %copy.15), channel_id=1, replica_groups=mesh['site'=16,'sector'=32] {'sector'}, dimensions={0} | all-to-all | bytes 2097152 | tf_op jit(solution)/shard_map/while/body/eval_jaxpr/all_to_all | solution.py:53
  241.1 12.2 %collective-permute-start = (bf16[1,128,128]{2,1,0:T(8,128)(2,1)S(1)}, bf16[1,128,128]{2,1,0:T(8,128)(2,1)S(1)}, u32[]{:S(2)}, u32[]{:S(2)}) collective-permute-start(bf16[1,128,128]{2,1,0:T(8,128)(2,1)S(1)} %bitcast.41), channel_id=1, source_target_pairs={{0,32},{32,64},{64,96},{96,128},{128,160},{160,192},{192,224},{224... | collective-permute-start | bytes 98312 | tf_op jit(solution)/shard_map/while/body/eval_jaxpr/ppermute | solution.py:10
  253.4 1.0 collective-permute-done
  256.3 24.2 %all_to_all.11 = bf16[32,128,128]{2,1,0:T(8,128)(2,1)S(1)} all-to-all(bf16[32,128,128]{2,1,0:T(8,128)(2,1)S(1)} %copy.15), channel_id=1, replica_groups=mesh['site'=16,'sector'=32] {'sector'}, dimensions={0} | all-to-all | bytes 2097152 | tf_op jit(solution)/shard_map/while/body/eval_jaxpr/all_to_all | solution.py:53
  280.7 12.9 %collective-permute-start = (bf16[1,128,128]{2,1,0:T(8,128)(2,1)S(1)}, bf16[1,128,128]{2,1,0:T(8,128)(2,1)S(1)}, u32[]{:S(2)}, u32[]{:S(2)}) collective-permute-start(bf16[1,128,128]{2,1,0:T(8,128)(2,1)S(1)} %bitcast.41), channel_id=1, source_target_pairs={{0,32},{32,64},{64,96},{96,128},{128,160},{160,192},{192,224},{224... | collective-permute-start | bytes 98312 | tf_op jit(solution)/shard_map/while/body/eval_jaxpr/ppermute | solution.py:10
  293.6 1.0 collective-permute-done
  296.6 23.4 %all_to_all.11 = bf16[32,128,128]{2,1,0:T(8,128)(2,1)S(1)} all-to-all(bf16[32,128,128]{2,1,0:T(8,128)(2,1)S(1)} %copy.15), channel_id=1, replica_groups=mesh['site'=16,'sector'=32] {'sector'}, dimensions={0} | all-to-all | bytes 2097152 | tf_op jit(solution)/shard_map/while/body/eval_jaxpr/all_to_all | solution.py:53
  320.1 12.5 %collective-permute-start = (bf16[1,128,128]{2,1,0:T(8,128)(2,1)S(1)}, bf16[1,128,128]{2,1,0:T(8,128)(2,1)S(1)}, u32[]{:S(2)}, u32[]{:S(2)}) collective-permute-start(bf16[1,128,128]{2,1,0:T(8,128)(2,1)S(1)} %bitcast.41), channel_id=1, source_target_pairs={{0,32},{32,64},{64,96},{96,128},{128,160},{160,192},{192,224},{224... | collective-permute-start | bytes 98312 | tf_op jit(solution)/shard_map/while/body/eval_jaxpr/ppermute | solution.py:10
  332.6 1.0 collective-permute-done
  335.6 24.0 %all_to_all.11 = bf16[32,128,128]{2,1,0:T(8,128)(2,1)S(1)} all-to-all(bf16[32,128,128]{2,1,0:T(8,128)(2,1)S(1)} %copy.15), channel_id=1, replica_groups=mesh['site'=16,'sector'=32] {'sector'}, dimensions={0} | all-to-all | bytes 2097152 | tf_op jit(solution)/shard_map/while/body/eval_jaxpr/all_to_all | solution.py:53
  359.8 11.7 %collective-permute-start = (bf16[1,128,128]{2,1,0:T(8,128)(2,1)S(1)}, bf16[1,128,128]{2,1,0:T(8,128)(2,1)S(1)}, u32[]{:S(2)}, u32[]{:S(2)}) collective-permute-start(bf16[1,128,128]{2,1,0:T(8,128)(2,1)S(1)} %bitcast.41), channel_id=1, source_target_pairs={{0,32},{32,64},{64,96},{96,128},{128,160},{160,192},{192,224},{224... | collective-permute-start | bytes 98312 | tf_op jit(solution)/shard_map/while/body/eval_jaxpr/ppermute | solution.py:10
  371.4 1.0 collective-permute-done
  374.4 24.7 %all_to_all.11 = bf16[32,128,128]{2,1,0:T(8,128)(2,1)S(1)} all-to-all(bf16[32,128,128]{2,1,0:T(8,128)(2,1)S(1)} %copy.15), channel_id=1, replica_groups=mesh['site'=16,'sector'=32] {'sector'}, dimensions={0} | all-to-all | bytes 2097152 | tf_op jit(solution)/shard_map/while/body/eval_jaxpr/all_to_all | solution.py:53
  399.3 11.0 %collective-permute-start = (bf16[1,128,128]{2,1,0:T(8,128)(2,1)S(1)}, bf16[1,128,128]{2,1,0:T(8,128)(2,1)S(1)}, u32[]{:S(2)}, u32[]{:S(2)}) collective-permute-start(bf16[1,128,128]{2,1,0:T(8,128)(2,1)S(1)} %bitcast.41), channel_id=1, source_target_pairs={{0,32},{32,64},{64,96},{96,128},{128,160},{160,192},{192,224},{224... | collective-permute-start | bytes 98312 | tf_op jit(solution)/shard_map/while/body/eval_jaxpr/ppermute | solution.py:10
  410.3 1.0 collective-permute-done
  413.2 25.4 %all_to_all.11 = bf16[32,128,128]{2,1,0:T(8,128)(2,1)S(1)} all-to-all(bf16[32,128,128]{2,1,0:T(8,128)(2,1)S(1)} %copy.15), channel_id=1, replica_groups=mesh['site'=16,'sector'=32] {'sector'}, dimensions={0} | all-to-all | bytes 2097152 | tf_op jit(solution)/shard_map/while/body/eval_jaxpr/all_to_all | solution.py:53
  438.9 10.3 %collective-permute-start = (bf16[1,128,128]{2,1,0:T(8,128)(2,1)S(1)}, bf16[1,128,128]{2,1,0:T(8,128)(2,1)S(1)}, u32[]{:S(2)}, u32[]{:S(2)}) collective-permute-start(bf16[1,128,128]{2,1,0:T(8,128)(2,1)S(1)} %bitcast.41), channel_id=1, source_target_pairs={{0,32},{32,64},{64,96},{96,128},{128,160},{160,192},{192,224},{224... | collective-permute-start | bytes 98312 | tf_op jit(solution)/shard_map/while/body/eval_jaxpr/ppermute | solution.py:10
  449.1 1.0 collective-permute-done
  452.1 26.2 %all_to_all.11 = bf16[32,128,128]{2,1,0:T(8,128)(2,1)S(1)} all-to-all(bf16[32,128,128]{2,1,0:T(8,128)(2,1)S(1)} %copy.15), channel_id=1, replica_groups=mesh['site'=16,'sector'=32] {'sector'}, dimensions={0} | all-to-all | bytes 2097152 | tf_op jit(solution)/shard_map/while/body/eval_jaxpr/all_to_all | solution.py:53
  478.4 9.5 %collective-permute-start = (bf16[1,128,128]{2,1,0:T(8,128)(2,1)S(1)}, bf16[1,128,128]{2,1,0:T(8,128)(2,1)S(1)}, u32[]{:S(2)}, u32[]{:S(2)}) collective-permute-start(bf16[1,128,128]{2,1,0:T(8,128)(2,1)S(1)} %bitcast.41), channel_id=1, source_target_pairs={{0,32},{32,64},{64,96},{96,128},{128,160},{160,192},{192,224},{224... | collective-permute-start | bytes 98312 | tf_op jit(solution)/shard_map/while/body/eval_jaxpr/ppermute | solution.py:10
  488.0 1.0 collective-permute-done
  490.9 26.8 %all_to_all.11 = bf16[32,128,128]{2,1,0:T(8,128)(2,1)S(1)} all-to-all(bf16[32,128,128]{2,1,0:T(8,128)(2,1)S(1)} %copy.15), channel_id=1, replica_groups=mesh['site'=16,'sector'=32] {'sector'}, dimensions={0} | all-to-all | bytes 2097152 | tf_op jit(solution)/shard_map/while/body/eval_jaxpr/all_to_all | solution.py:53
  517.8 8.9 %collective-permute-start = (bf16[1,128,128]{2,1,0:T(8,128)(2,1)S(1)}, bf16[1,128,128]{2,1,0:T(8,128)(2,1)S(1)}, u32[]{:S(2)}, u32[]{:S(2)}) collective-permute-start(bf16[1,128,128]{2,1,0:T(8,128)(2,1)S(1)} %bitcast.41), channel_id=1, source_target_pairs={{0,32},{32,64},{64,96},{96,128},{128,160},{160,192},{192,224},{224... | collective-permute-start | bytes 98312 | tf_op jit(solution)/shard_map/while/body/eval_jaxpr/ppermute | solution.py:10
  526.8 1.0 collective-permute-done
  529.8 27.6 %all_to_all.11 = bf16[32,128,128]{2,1,0:T(8,128)(2,1)S(1)} all-to-all(bf16[32,128,128]{2,1,0:T(8,128)(2,1)S(1)} %copy.15), channel_id=1, replica_groups=mesh['site'=16,'sector'=32] {'sector'}, dimensions={0} | all-to-all | bytes 2097152 | tf_op jit(solution)/shard_map/while/body/eval_jaxpr/all_to_all | solution.py:53
  557.5 8.1 %collective-permute-start = (bf16[1,128,128]{2,1,0:T(8,128)(2,1)S(1)}, bf16[1,128,128]{2,1,0:T(8,128)(2,1)S(1)}, u32[]{:S(2)}, u32[]{:S(2)}) collective-permute-start(bf16[1,128,128]{2,1,0:T(8,128)(2,1)S(1)} %bitcast.41), channel_id=1, source_target_pairs={{0,32},{32,64},{64,96},{96,128},{128,160},{160,192},{192,224},{224... | collective-permute-start | bytes 98312 | tf_op jit(solution)/shard_map/while/body/eval_jaxpr/ppermute | solution.py:10
  565.6 1.0 collective-permute-done
  568.6 28.3 %all_to_all.11 = bf16[32,128,128]{2,1,0:T(8,128)(2,1)S(1)} all-to-all(bf16[32,128,128]{2,1,0:T(8,128)(2,1)S(1)} %copy.15), channel_id=1, replica_groups=mesh['site'=16,'sector'=32] {'sector'}, dimensions={0} | all-to-all | bytes 2097152 | tf_op jit(solution)/shard_map/while/body/eval_jaxpr/all_to_all | solution.py:53
  597.0 7.4 %collective-permute-start = (bf16[1,128,128]{2,1,0:T(8,128)(2,1)S(1)}, bf16[1,128,128]{2,1,0:T(8,128)(2,1)S(1)}, u32[]{:S(2)}, u32[]{:S(2)}) collective-permute-start(bf16[1,128,128]{2,1,0:T(8,128)(2,1)S(1)} %bitcast.41), channel_id=1, source_target_pairs={{0,32},{32,64},{64,96},{96,128},{128,160},{160,192},{192,224},{224... | collective-permute-start | bytes 98312 | tf_op jit(solution)/shard_map/while/body/eval_jaxpr/ppermute | solution.py:10
  604.5 1.0 collective-permute-done
  (104 shorter events, 32.8 us)
Async XLA Ops:
  0.0 3.0 copy-start
  1.4 0.7 copy-start.2
  1.4 0.7 copy-start.3
  2.3 0.7 copy-start.4
  2.3 0.7 copy-start.5
  41.1 8.3 %collective-permute-start = (bf16[1,128,128]{2,1,0:T(8,128)(2,1)S(1)}, bf16[1,128,128]{2,1,0:T(8,128)(2,1)S(1)}, u32[]{:S(2)}, u32[]{:S(2)}) collective-permute-start(bf16[1,128,128]{2,1,0:T(8,128)(2,1)S(1)} %bitcast.41), channel_id=1, source_target_pairs={{0,32},{32,64},{64,96},{96,128},{128,160},{160,192},{192,224},{224... | collective-permute-start | bytes 98312 | tf_op jit(solution)/shard_map/while/body/eval_jaxpr/ppermute | solution.py:10
  82.8 7.6 %collective-permute-start = (bf16[1,128,128]{2,1,0:T(8,128)(2,1)S(1)}, bf16[1,128,128]{2,1,0:T(8,128)(2,1)S(1)}, u32[]{:S(2)}, u32[]{:S(2)}) collective-permute-start(bf16[1,128,128]{2,1,0:T(8,128)(2,1)S(1)} %bitcast.41), channel_id=1, source_target_pairs={{0,32},{32,64},{64,96},{96,128},{128,160},{160,192},{192,224},{224... | collective-permute-start | bytes 98312 | tf_op jit(solution)/shard_map/while/body/eval_jaxpr/ppermute | solution.py:10
  122.5 9.1 %collective-permute-start = (bf16[1,128,128]{2,1,0:T(8,128)(2,1)S(1)}, bf16[1,128,128]{2,1,0:T(8,128)(2,1)S(1)}, u32[]{:S(2)}, u32[]{:S(2)}) collective-permute-start(bf16[1,128,128]{2,1,0:T(8,128)(2,1)S(1)} %bitcast.41), channel_id=1, source_target_pairs={{0,32},{32,64},{64,96},{96,128},{128,160},{160,192},{192,224},{224... | collective-permute-start | bytes 98312 | tf_op jit(solution)/shard_map/while/body/eval_jaxpr/ppermute | solution.py:10
  162.0 11.1 %collective-permute-start = (bf16[1,128,128]{2,1,0:T(8,128)(2,1)S(1)}, bf16[1,128,128]{2,1,0:T(8,128)(2,1)S(1)}, u32[]{:S(2)}, u32[]{:S(2)}) collective-permute-start(bf16[1,128,128]{2,1,0:T(8,128)(2,1)S(1)} %bitcast.41), channel_id=1, source_target_pairs={{0,32},{32,64},{64,96},{96,128},{128,160},{160,192},{192,224},{224... | collective-permute-start | bytes 98312 | tf_op jit(solution)/shard_map/while/body/eval_jaxpr/ppermute | solution.py:10
  201.5 12.6 %collective-permute-start = (bf16[1,128,128]{2,1,0:T(8,128)(2,1)S(1)}, bf16[1,128,128]{2,1,0:T(8,128)(2,1)S(1)}, u32[]{:S(2)}, u32[]{:S(2)}) collective-permute-start(bf16[1,128,128]{2,1,0:T(8,128)(2,1)S(1)} %bitcast.41), channel_id=1, source_target_pairs={{0,32},{32,64},{64,96},{96,128},{128,160},{160,192},{192,224},{224... | collective-permute-start | bytes 98312 | tf_op jit(solution)/shard_map/while/body/eval_jaxpr/ppermute | solution.py:10
  241.1 13.2 %collective-permute-start = (bf16[1,128,128]{2,1,0:T(8,128)(2,1)S(1)}, bf16[1,128,128]{2,1,0:T(8,128)(2,1)S(1)}, u32[]{:S(2)}, u32[]{:S(2)}) collective-permute-start(bf16[1,128,128]{2,1,0:T(8,128)(2,1)S(1)} %bitcast.41), channel_id=1, source_target_pairs={{0,32},{32,64},{64,96},{96,128},{128,160},{160,192},{192,224},{224... | collective-permute-start | bytes 98312 | tf_op jit(solution)/shard_map/while/body/eval_jaxpr/ppermute | solution.py:10
  280.7 13.9 %collective-permute-start = (bf16[1,128,128]{2,1,0:T(8,128)(2,1)S(1)}, bf16[1,128,128]{2,1,0:T(8,128)(2,1)S(1)}, u32[]{:S(2)}, u32[]{:S(2)}) collective-permute-start(bf16[1,128,128]{2,1,0:T(8,128)(2,1)S(1)} %bitcast.41), channel_id=1, source_target_pairs={{0,32},{32,64},{64,96},{96,128},{128,160},{160,192},{192,224},{224... | collective-permute-start | bytes 98312 | tf_op jit(solution)/shard_map/while/body/eval_jaxpr/ppermute | solution.py:10
  320.1 13.5 %collective-permute-start = (bf16[1,128,128]{2,1,0:T(8,128)(2,1)S(1)}, bf16[1,128,128]{2,1,0:T(8,128)(2,1)S(1)}, u32[]{:S(2)}, u32[]{:S(2)}) collective-permute-start(bf16[1,128,128]{2,1,0:T(8,128)(2,1)S(1)} %bitcast.41), channel_id=1, source_target_pairs={{0,32},{32,64},{64,96},{96,128},{128,160},{160,192},{192,224},{224... | collective-permute-start | bytes 98312 | tf_op jit(solution)/shard_map/while/body/eval_jaxpr/ppermute | solution.py:10
  359.8 12.7 %collective-permute-start = (bf16[1,128,128]{2,1,0:T(8,128)(2,1)S(1)}, bf16[1,128,128]{2,1,0:T(8,128)(2,1)S(1)}, u32[]{:S(2)}, u32[]{:S(2)}) collective-permute-start(bf16[1,128,128]{2,1,0:T(8,128)(2,1)S(1)} %bitcast.41), channel_id=1, source_target_pairs={{0,32},{32,64},{64,96},{96,128},{128,160},{160,192},{192,224},{224... | collective-permute-start | bytes 98312 | tf_op jit(solution)/shard_map/while/body/eval_jaxpr/ppermute | solution.py:10
  399.3 12.0 %collective-permute-start = (bf16[1,128,128]{2,1,0:T(8,128)(2,1)S(1)}, bf16[1,128,128]{2,1,0:T(8,128)(2,1)S(1)}, u32[]{:S(2)}, u32[]{:S(2)}) collective-permute-start(bf16[1,128,128]{2,1,0:T(8,128)(2,1)S(1)} %bitcast.41), channel_id=1, source_target_pairs={{0,32},{32,64},{64,96},{96,128},{128,160},{160,192},{192,224},{224... | collective-permute-start | bytes 98312 | tf_op jit(solution)/shard_map/while/body/eval_jaxpr/ppermute | solution.py:10
  438.9 11.3 %collective-permute-start = (bf16[1,128,128]{2,1,0:T(8,128)(2,1)S(1)}, bf16[1,128,128]{2,1,0:T(8,128)(2,1)S(1)}, u32[]{:S(2)}, u32[]{:S(2)}) collective-permute-start(bf16[1,128,128]{2,1,0:T(8,128)(2,1)S(1)} %bitcast.41), channel_id=1, source_target_pairs={{0,32},{32,64},{64,96},{96,128},{128,160},{160,192},{192,224},{224... | collective-permute-start | bytes 98312 | tf_op jit(solution)/shard_map/while/body/eval_jaxpr/ppermute | solution.py:10
  478.4 10.6 %collective-permute-start = (bf16[1,128,128]{2,1,0:T(8,128)(2,1)S(1)}, bf16[1,128,128]{2,1,0:T(8,128)(2,1)S(1)}, u32[]{:S(2)}, u32[]{:S(2)}) collective-permute-start(bf16[1,128,128]{2,1,0:T(8,128)(2,1)S(1)} %bitcast.41), channel_id=1, source_target_pairs={{0,32},{32,64},{64,96},{96,128},{128,160},{160,192},{192,224},{224... | collective-permute-start | bytes 98312 | tf_op jit(solution)/shard_map/while/body/eval_jaxpr/ppermute | solution.py:10
  517.8 9.9 %collective-permute-start = (bf16[1,128,128]{2,1,0:T(8,128)(2,1)S(1)}, bf16[1,128,128]{2,1,0:T(8,128)(2,1)S(1)}, u32[]{:S(2)}, u32[]{:S(2)}) collective-permute-start(bf16[1,128,128]{2,1,0:T(8,128)(2,1)S(1)} %bitcast.41), channel_id=1, source_target_pairs={{0,32},{32,64},{64,96},{96,128},{128,160},{160,192},{192,224},{224... | collective-permute-start | bytes 98312 | tf_op jit(solution)/shard_map/while/body/eval_jaxpr/ppermute | solution.py:10
  557.5 9.1 %collective-permute-start = (bf16[1,128,128]{2,1,0:T(8,128)(2,1)S(1)}, bf16[1,128,128]{2,1,0:T(8,128)(2,1)S(1)}, u32[]{:S(2)}, u32[]{:S(2)}) collective-permute-start(bf16[1,128,128]{2,1,0:T(8,128)(2,1)S(1)} %bitcast.41), channel_id=1, source_target_pairs={{0,32},{32,64},{64,96},{96,128},{128,160},{160,192},{192,224},{224... | collective-permute-start | bytes 98312 | tf_op jit(solution)/shard_map/while/body/eval_jaxpr/ppermute | solution.py:10
  597.0 8.4 %collective-permute-start = (bf16[1,128,128]{2,1,0:T(8,128)(2,1)S(1)}, bf16[1,128,128]{2,1,0:T(8,128)(2,1)S(1)}, u32[]{:S(2)}, u32[]{:S(2)}) collective-permute-start(bf16[1,128,128]{2,1,0:T(8,128)(2,1)S(1)} %bitcast.41), channel_id=1, source_target_pairs={{0,32},{32,64},{64,96},{96,128},{128,160},{160,192},{192,224},{224... | collective-permute-start | bytes 98312 | tf_op jit(solution)/shard_map/while/body/eval_jaxpr/ppermute | solution.py:10
  605.5 0.6 copy-start.1
where the time goes:
time: 608 us; the launch traced here: 606 us
  blocking collectives  407 us (67%)
  starting transfers between devices  148 us (24%)
  matrix products  16.1 us (3%)
  local copies, waits for them, and re-layouts  15.9 us (3%)
  waiting for transfers between devices  14.9 us (2%)
    all_to_all x15, blocking collectives, section(): lax.all_to_all(partial_value, 'sector', split_axis=0, concat_axis=0, tile...  407 us
    ppermute x15, starting transfers between devices, from_behind(): return lax.ppermute(x, axis, pairs)  148 us
    ppermute x15, waiting for transfers between devices, from_behind(): return lax.ppermute(x, axis, pairs)  14.9 us
  transfers between devices with their start and end apart: 15, of which 15 were waited for; matrix products, arithmetic and copies ran while one was open for 0% of the time, Pallas kernels for 0%

commit v1 on v0

v1 whole, which is shorter than its diff:
```python
import functools

import jax
import jax.numpy as jnp
from jax import lax
from jax.experimental import pallas as pl
from jax.experimental.pallas import tpu as pltpu
from jax.sharding import PartitionSpec as P

MESH = pl.DeviceIdType.MESH
BF16 = jnp.bfloat16
F32 = jnp.float32

NX, NY, NZ = 4, 8, 8
SLOTS = NX * NY
STEPS = 15
TRIP = 16
ROWS = 16
TILE = 128


def hops(offset):
    dy, dx = offset
    return min(dy, NY - dy) + min(dx, NX - dx)


PLANE = sorted(
    [(dy, dx) for dy in range(NY) for dx in range(NX) if (dy, dx) != (0, 0)], key=hops, reverse=True
)
COLUMN = sorted(range(1, NZ), key=lambda d: min(d, NZ - d), reverse=True)
N_PLANE = len(PLANE)
N_COLUMN = len(COLUMN)


def chain(
    env_ref, bt_ref, ket_ref, first_ref, second_ref, weight_ref, out_ref,
    env, prod, part, got, leave, land,
    part_send, part_recv, env_send, env_recv, out_send, out_recv,
):
    site = lax.axis_index("site")
    sector = lax.axis_index("sector")
    z, core = site // 2, lax.rem(site, 2)
    y, x = sector // NX, lax.rem(sector, NX)

    def slot_at(offset):
        return lax.rem(y + offset[0], NY) * NX + lax.rem(x + offset[1], NX)

    def site_at(d):
        return lax.rem(z + d, NZ) * 2 + 1

    barrier = pltpu.get_barrier_semaphore()
    pl.semaphore_signal(barrier, inc=1, device_id=(z * 2 + 1 - core, sector), device_id_type=MESH)

    @pl.when(core == 0)
    def _():
        pl.semaphore_wait(barrier, 1)

        @pl.when(z == 0)
        def _():
            out_ref[...] = env_ref[...]

        @pl.when(z > 0)
        def _():
            pltpu.make_async_remote_copy(
                src_ref=leave, dst_ref=land, send_sem=out_send, recv_sem=out_recv,
                device_id=(site + 1, sector), device_id_type=MESH,
            ).wait_recv()
            out_ref[...] = land[...]

    @pl.when(core == 1)
    def _():
        for offset in PLANE:
            pl.semaphore_signal(barrier, inc=1, device_id=(site, slot_at(offset)), device_id_type=MESH)
        for d in COLUMN:
            pl.semaphore_signal(barrier, inc=1, device_id=(site_at(d), sector), device_id_type=MESH)
        pl.semaphore_wait(barrier, 1 + N_PLANE + N_COLUMN)

        env[0] = env_ref[...]
        prod[TRIP] = jnp.zeros((ROWS, TILE), F32)
        rows = pl.ds(pl.multiple_of(z * ROWS, ROWS), ROWS)

        def send_part(p, i):
            return pltpu.make_async_remote_copy(
                src_ref=part.at[p, i], dst_ref=got.at[p, i],
                send_sem=part_send.at[p], recv_sem=part_recv.at[p],
                device_id=(site, slot_at(PLANE[i])), device_id_type=MESH,
            )

        def all_parts(p):
            return pltpu.make_async_remote_copy(
                src_ref=part.at[p, pl.ds(0, N_PLANE)], dst_ref=got.at[p, pl.ds(0, N_PLANE)],
                send_sem=part_send.at[p], recv_sem=part_recv.at[p],
                device_id=(site, slot_at(PLANE[0])), device_id_type=MESH,
            )

        def send_rows(q, d):
            return pltpu.make_async_remote_copy(
                src_ref=env.at[q, rows], dst_ref=env.at[q, rows],
                send_sem=env_send.at[q], recv_sem=env_recv.at[q],
                device_id=(site_at(d), sector), device_id_type=MESH,
            )

        def all_rows(q):
            span = pl.ds(0, N_COLUMN * ROWS)
            return pltpu.make_async_remote_copy(
                src_ref=env.at[q, span], dst_ref=env.at[q, span],
                send_sem=env_send.at[q], recv_sem=env_recv.at[q],
                device_id=(site_at(COLUMN[0]), sector), device_id_type=MESH,
            )

        def to_core_0():
            return pltpu.make_async_remote_copy(
                src_ref=leave, dst_ref=land, send_sem=out_send, recv_sem=out_recv,
                device_id=(z * 2, sector), device_id_type=MESH,
            )

        def step(j, carry):
            p = lax.rem(j, 2)

            @pl.when(j > 0)
            def _():
                all_rows(p).wait_recv()

            left = jnp.dot(bt_ref[j], env[p], preferred_element_type=F32)
            for k in range(TRIP):
                scaled = (left[k * ROWS:(k + 1) * ROWS] * weight_ref[j * TRIP + k]).astype(BF16)
                prod[k] = jnp.dot(scaled, ket_ref[j, k], preferred_element_type=F32)

            def summed(slot):
                at = j * SLOTS + slot
                return (prod[first_ref[at]] + prod[second_ref[at]]).astype(BF16)

            for i in range(N_PLANE):
                part[p, i] = summed(slot_at(PLANE[i]))
                send_part(p, i).start()
            got[p, N_PLANE] = summed(sector)

            @pl.when(j > 0)
            def _():
                all_parts(1 - p).wait_send()
                all_rows(p).wait_send()

            @pl.when((j > 0) & (j == z * 2))
            def _():
                leave[...] = env[p]
                to_core_0().start()

            @pl.when(j == site)
            def _():
                out_ref[...] = env[p]

            all_parts(p).wait_recv()
            total = got[p, 0].astype(F32)
            for i in range(1, SLOTS):
                total += got[p, i].astype(F32)
            env[1 - p, rows] = total.astype(BF16)
            for d in COLUMN:
                send_rows(1 - p, d).start()
            return carry

        lax.fori_loop(0, STEPS, step, 0)
        last = STEPS % 2
        all_rows(last).wait_recv()

        @pl.when(site == STEPS)
        def _():
            out_ref[...] = env[last]

        all_rows(last).wait_send()
        all_parts(1 - last).wait_send()

        @pl.when(z > 0)
        def _():
            to_core_0().wait_send()


def run_chain(env, bt, ket, first, second, weight):
    vmem = pl.BlockSpec(memory_space=pltpu.VMEM)
    smem = pl.BlockSpec(memory_space=pltpu.SMEM)
    dma = pltpu.SemaphoreType.DMA
    return pl.pallas_call(
        chain,
        out_shape=jax.ShapeDtypeStruct((TILE, TILE), BF16),
        in_specs=[vmem, vmem, vmem, smem, smem, smem],
        out_specs=vmem,
        scratch_shapes=[
            pltpu.VMEM((2, TILE, TILE), BF16),
            pltpu.VMEM((TRIP + 1, ROWS, TILE), F32),
            pltpu.VMEM((2, N_PLANE, ROWS, TILE), BF16),
            pltpu.VMEM((2, SLOTS, ROWS, TILE), BF16),
            pltpu.VMEM((TILE, TILE), BF16),
            pltpu.VMEM((TILE, TILE), BF16),
            dma((2,)), dma((2,)), dma((2,)), dma((2,)), dma, dma,
        ],
        compiler_params=pltpu.CompilerParams(
            collective_id=0, has_side_effects=True, vmem_limit_bytes=40 << 20
        ),
        name="chain",
    )(env, bt, ket, first, second, weight)


def lookups(joining_out, joining_mpo, owner, mpo_weight):
    slots = jnp.arange(SLOTS, dtype=jnp.int32)
    outputs = joining_out[0, :, 0]
    target = jnp.sum(jnp.where(outputs[:, None] == slots[None, :], owner[None, :], 0), axis=1)
    terms = jnp.arange(mpo_weight.shape[1], dtype=jnp.int32)
    weights = jnp.sum(
        jnp.where(joining_mpo[0][:, None] == terms[None, :], mpo_weight[0][None, :], 0.0), axis=1
    )
    place = jnp.arange(TRIP, dtype=jnp.int32)[:, None]
    hit = target[:, None] == slots[None, :]
    first = jnp.min(jnp.where(hit, place, TRIP), axis=0)
    second = jnp.min(jnp.where(hit & (place != first[None, :]), place, TRIP), axis=0)
    return first, second, weights


def local(left_env, mps_bra, mps_ket, joining_out, joining_mpo, owner, mpo_weight):
    first, second, weights = lookups(joining_out, joining_mpo, owner, mpo_weight)
    tables = lax.all_gather(jnp.concatenate([first, second]), "site")
    first, second = tables[:, :SLOTS].reshape(-1), tables[:, SLOTS:].reshape(-1)
    weights = lax.all_gather(weights, "site").reshape(-1)
    ket = lax.all_gather(mps_ket[0], "site")
    bt = mps_bra[0].transpose(0, 2, 1).reshape(TRIP, NZ, ROWS, TILE).transpose(1, 0, 2, 3)
    bt = jnp.repeat(bt.reshape(NZ, TRIP * ROWS, TILE), 2, axis=0)
    bt = lax.all_to_all(bt, "site", split_axis=0, concat_axis=0, tiled=True)
    return run_chain(left_env[0], bt, ket, first, second, weights)[None, None]


def solution(mesh):
    return jax.shard_map(
        local,
        mesh=mesh,
        in_specs=(
            P("sector", None, None),
            P("site", "sector", None, None),
            P("site", "sector", None, None),
            P("site", "sector", None),
            P("site", "sector"),
            P(),
            P("site", None),
        ),
        out_specs=P("site", "sector", None, None),
        check_vma=False,
    )
```

time: 608 us -> 247 us (0.41)
  blocking collectives: 407 us -> 62.7 us
  Pallas kernels: 0 us -> 146 us
  starting transfers between devices: 148 us -> 11.8 us
  matrix products: 16.1 us -> 0 us
  between operations: 0.06 us -> 14.7 us
  waiting for transfers between devices: 14.9 us -> 1.08 us
  local copies, waits for them, and re-layouts: 15.9 us -> 9.18 us
    all_to_all x15 -> x0, blocking collectives: 407 us -> none  [section(): lax.all_to_all(partial_value, 'sector', split_axis=0, concat_axis=0, tile...]
    ppermute x15 -> x0, starting transfers between devices: 148 us -> none  [from_behind(): return lax.ppermute(x, axis, pairs)]
    pallas_call x0 -> x1, Pallas kernels: none -> 146 us  [run_chain(): pl.pallas_call(chain, out_shape=jax.ShapeDtypeStruct((TILE, TILE), BF16),...]
    unnamed x0 -> x2, blocking collectives: none -> 62.7 us
    dot_general x30 -> x0, matrix products: 16.1 us -> none  [the longest x15 8.07 us: triple_sums(): jnp.einsum('kai,kac->kic', mps_bra[0], inner_part, preferred_element_type...]
    ppermute x15 -> x0, waiting for transfers between devices: 14.9 us -> none  [from_behind(): return lax.ppermute(x, axis, pairs)]
    all_to_all x0 -> x1, starting transfers between devices: none -> 11.8 us  [local(): bt = lax.all_to_all(bt, 'site', split_axis=0, concat_axis=0, tiled=True)]
    dot_general x15 -> x0, local copies, waits for them, and re-layouts: 6.44 us -> none  [triple_sums(): jnp.einsum('kai,kac->kic', mps_bra[0], inner_part, preferred_element_type...]
  transfers between devices with their start and end apart: 15 -> 2, of which waited for: 15 -> 1; matrix products, arithmetic and copies ran while one was open for 0% -> 3% of each run, Pallas kernels for 0% -> 0%
where the time goes in v1:
time: 247 us
  Pallas kernels  146 us (59%)
  blocking collectives  62.7 us (25%)
  between operations  14.7 us (6%)
  starting transfers between devices  11.8 us (5%)
  local copies, waits for them, and re-layouts  9.18 us (4%)
    pallas_call x1, Pallas kernels, run_chain(): pl.pallas_call(chain, out_shape=jax.ShapeDtypeStruct((TILE, TILE), BF16),...  146 us
    unnamed x2, blocking collectives  62.7 us
    all_to_all x1, starting transfers between devices, local(): bt = lax.all_to_all(bt, 'site', split_axis=0, concat_axis=0, tiled=True)  11.8 us
    unnamed x10, local copies, waits for them, and re-layouts  7.57 us
  transfers between devices with their start and end apart: 2, of which 1 were waited for; matrix products, arithmetic and copies ran while one was open for 3% of the time, Pallas kernels for 0%

profile of v1, /device:TPU:1, one launch (start us, length us, event | category | flops | bytes accessed | tf_op | source)
XLA Modules:
  0.0 247.0 jit_solution(11878934450598841849)
XLA Ops:
  6.5 0.0 all-gather.4.cloned.1.call-start
  6.5 0.7 all-gather.4.cloned.1.call-update
  7.3 1.3 copy.12
  8.6 1.3 broadcast_in_dim.59
  9.9 11.8 %all-to-all-start = ((bf16[16,256,128]{2,1,0:T(8,128)(2,1)}), bf16[16,256,128]{2,1,0:T(8,128)(2,1)S(1)}, u32[]{:S(2)}, u32[]{:S(2)}) async-start(bf16[16,256,128]{2,1,0:T(8,128)(2,1)} %bitcast.6), calls=%async_computation | async-start | bytes 2097152 | tf_op jit(solution)/shard_map/all_to_all | solution.py:225
  21.7 1.3 dynamic-slice
  23.6 0.9 select_reduce_fusion.2
  24.5 0.1 select_reduce_fusion.1
  24.6 0.1 select_reduce_fusion
  24.7 0.2 add_dynamic-update-slice_fusion
  24.9 37.4 %all-reduce = s32[1024]{0:T(1024)S(1)} all-reduce(s32[1024]{0:T(1024)S(1)} %add_dynamic-update-slice_fusion), channel_id=2, replica_groups=mesh['site'=16,'sector'=32] {'site'}, use_global_device_ids=true, to_apply=%add | all-reduce | flops 1024 | bytes 8192
  62.2 0.1 reshape.29
  62.3 0.1 fusion.1
  62.4 0.1 reshape.26.first_ref
  62.5 0.1 reshape.27.second_ref
  63.2 0.8 select_reduce_fusion.3
  63.9 0.2 dynamic-update-slice.1
  64.2 25.3 %all-reduce.1.weight_ref = f32[256]{0:T(256)S(1)} all-reduce(f32[256]{0:T(256)S(1)} %dynamic-update-slice.1), channel_id=3, replica_groups=mesh['site'=16,'sector'=32] {'site'}, use_global_device_ids=true, to_apply=%add.1 | all-reduce | flops 256 | bytes 2048
  89.5 0.0 all-to-all-done.bt_ref
  89.5 0.4 all-gather.4.cloned.1.call-done.ket_ref
  89.9 0.0 copy-start
  89.9 3.4 %copy-done = bf16[16,16,128,128]{3,2,1,0:T(8,128)(2,1)S(1)} copy-done((bf16[16,16,128,128]{3,2,1,0:T(8,128)(2,1)S(1)}, bf16[16,16,128,128]{3,2,1,0:T(8,128)(2,1)}, u32[]{:S(2)}) %copy-start) | copy-done | bytes 8388632
  93.2 0.0 copy-start.1
  93.2 0.8 copy-done.1
  94.0 145.5 %chain.1 = bf16[128,128]{1,0:T(8,128)(2,1)S(1)} custom-call(bf16[128,128]{1,0:T(8,128)(2,1)S(1)} %bitcast.17, bf16[16,256,128]{2,1,0:T(8,128)(2,1)S(1)} %all-to-all-done.bt_ref, bf16[16,16,128,128]{3,2,1,0:T(8,128)(2,1)S(1)} %copy-done, s32[512]{0:T(512)S(1)} %reshape.26.first_ref, s32[512]{0:T(512)S(1)} %reshape.27.second_ref, f32[256]{0:T(256)S(1)} %all-reduce.1.weight_ref), custom_call_target="tpu_custom_call" | custom-call | tf_op jit(solution)/shard_map/chain/pallas_call | solution.py:181
  239.5 0.6 copy.17
  (3 shorter events, 0.0 us)
Async XLA Ops:
  6.5 83.3 %all-gather.4.cloned.1.call-start = ((), (), s32[]{:S(2)}) async-start(), calls=%async_computation.1 | async-start | bytes 8912896 | tf_op jit(solution)/shard_map/all_gather | solution.py:222
  9.9 79.6 %all-to-all-start = ((bf16[16,256,128]{2,1,0:T(8,128)(2,1)}), bf16[16,256,128]{2,1,0:T(8,128)(2,1)S(1)}, u32[]{:S(2)}, u32[]{:S(2)}) async-start(bf16[16,256,128]{2,1,0:T(8,128)(2,1)} %bitcast.6), calls=%async_computation | async-start | bytes 2097152 | tf_op jit(solution)/shard_map/all_to_all | solution.py:225
  89.9 3.4 %copy-start = (bf16[16,16,128,128]{3,2,1,0:T(8,128)(2,1)S(1)}, bf16[16,16,128,128]{3,2,1,0:T(8,128)(2,1)}, u32[]{:S(2)}) copy-start(bf16[16,16,128,128]{3,2,1,0:T(8,128)(2,1)} %all-gather.4.cloned.1.call-done.ket_ref) | copy-start | bytes 25165828
  93.2 0.8 copy-start.1
Sparse Core Ops, SparseCore 0:
  9.5 80.3 all-gather.3

commit v2 on v1

v2 whole, which is shorter than its diff:
```python
import functools

import jax
import jax.numpy as jnp
from jax import lax
from jax.experimental import pallas as pl
from jax.experimental.pallas import tpu as pltpu
from jax.sharding import PartitionSpec as P

MESH = pl.DeviceIdType.MESH
BF16 = jnp.bfloat16
F32 = jnp.float32

NX, NY, NZ = 4, 8, 8
SLOTS = NX * NY
STEPS = 15
TRIP = 16
ROWS = 16
TILE = 128
PIECES = 4
PIECE = TRIP // PIECES


def hops(offset):
    dy, dx = offset
    return min(dy, NY - dy) + min(dx, NX - dx)


PLANE = sorted(
    [(dy, dx) for dy in range(NY) for dx in range(NX) if (dy, dx) != (0, 0)], key=hops, reverse=True
)
COLUMN = sorted(range(1, NZ), key=lambda d: min(d, NZ - d), reverse=True)
N_PLANE = len(PLANE)
N_COLUMN = len(COLUMN)


def chain(
    env_ref, bra_ref, ket_ref, table_ref, weight_ref, out_ref,
    env, prod, part, got, leave, land, bt_out, bt, first_out, first_in, kets, tables, lookup,
    part_send, part_recv, env_send, env_recv, out_send, out_recv, bt_send, bt_recv,
    first_send, first_recv, table_send, table_recv, local_sem,
    up_send, down_send, over_send, ket_recv,
):
    site = lax.axis_index("site")
    sector = lax.axis_index("sector")
    z, core = site // 2, lax.rem(site, 2)
    y, x = sector // NX, lax.rem(sector, NX)
    rows = pl.ds(pl.multiple_of(z * ROWS, ROWS), ROWS)

    def slot_at(offset):
        return lax.rem(y + offset[0], NY) * NX + lax.rem(x + offset[1], NX)

    def plane_at(d):
        return lax.rem(z + d, NZ)

    def remote(src, dst, send_sem, recv_sem, to_site, to_sector=sector):
        return pltpu.make_async_remote_copy(
            src_ref=src, dst_ref=dst, send_sem=send_sem, recv_sem=recv_sem,
            device_id=(to_site, to_sector), device_id_type=MESH,
        )

    barrier = pltpu.get_barrier_semaphore()

    def greet(to_site, to_sector=sector):
        pl.semaphore_signal(barrier, inc=1, device_id=(to_site, to_sector), device_id_type=MESH)

    def send_table(d):
        return remote(tables.at[site], tables.at[site], table_send, table_recv, plane_at(d) * 2 + 1)

    def send_bt(d):
        return remote(
            bt_out.at[plane_at(d)], bt.at[site], bt_send, bt_recv.at[site], plane_at(d) * 2 + 1
        )

    def send_first(d):
        return remote(
            first_out.at[plane_at(d)], first_in, first_send, first_recv, plane_at(d) * 2 + 1
        )

    def to_core_0():
        return remote(leave, land, out_send, out_recv, z * 2)

    def ket_piece(f, q, send_sem, to_site):
        held = kets.at[f, pl.ds(q * PIECE, PIECE)]
        return remote(held, held, send_sem, ket_recv.at[f, q], to_site)

    def whole_ket(f, send_sem):
        return remote(kets.at[f], kets.at[f], send_sem, ket_recv.at[f, 0], site + 1 - 2 * core)

    greet(z * 2 + 1 - core)
    for d in COLUMN:
        greet(plane_at(d) * 2 + 1)

    @pl.when(core == 0)
    def _():
        greet(plane_at(1) * 2)
        greet(plane_at(NZ - 1) * 2)

    @pl.when(core == 1)
    def _():
        for d in COLUMN:
            greet(plane_at(d) * 2)
        for offset in PLANE:
            greet(site, slot_at(offset))

    own_ket = pltpu.make_async_copy(ket_ref, kets.at[site], local_sem)
    own_ket.start()
    tables[site] = table_ref[...]
    for k in range(TRIP):
        turned = jnp.transpose(bra_ref[k].astype(F32)) * weight_ref[k]
        bt_out[:, k * ROWS:(k + 1) * ROWS, :] = turned.astype(BF16).reshape(NZ, ROWS, TILE)

    @pl.when(core == 0)
    def _():
        @pl.when(z == 0)
        def _():
            out_ref[...] = env_ref[...]
            for k in range(TRIP):
                span = pl.ds(k * ROWS, ROWS)
                left = jnp.dot(
                    bt_out[:, span, :].reshape(TILE, TILE), env_ref[...], preferred_element_type=F32
                )
                whole = jnp.dot(left.astype(BF16), ket_ref[k], preferred_element_type=F32)
                first_out[:, span, :] = whole.astype(BF16).reshape(NZ, ROWS, TILE)

        pl.semaphore_wait(barrier, N_COLUMN + 3)
        own_ket.wait()
        for d in COLUMN + [0]:
            send_table(d).start()

        @pl.when(z == 0)
        def _():
            for d in COLUMN + [0]:
                send_first(d).start()

        def ways(f):
            away = lax.rem(z - f // 2 + NZ, NZ)
            up = away < NZ // 2
            down = (away == 0) | (away > NZ // 2 + 1)
            over = (away > 0) | (f == site)
            return up, down, over

        def serve(f, carry):
            up, down, over = ways(f)

            @pl.when(f == site)
            def _():
                for d in COLUMN + [0]:
                    send_bt(d).start()

            for q in range(PIECES):
                @pl.when(f != site)
                def _():
                    ket_piece(f, q, up_send, z * 2 + 1).wait_recv()

                @pl.when(up)
                def _():
                    ket_piece(f, q, up_send, plane_at(1) * 2).start()

                @pl.when(down)
                def _():
                    ket_piece(f, q, down_send, plane_at(NZ - 1) * 2).start()

                @pl.when(over)
                def _():
                    held = kets.at[f, pl.ds(q * PIECE, PIECE)]
                    remote(held, held, over_send, ket_recv.at[f, 0], z * 2 + 1).start()
            return carry

        lax.fori_loop(1, STEPS, serve, 0)

        @pl.when(z > 0)
        def _():
            to_core_0().wait_recv()
            out_ref[...] = land[...]

        def settle(f, carry):
            up, down, over = ways(f)
            for way, sem in ((up, up_send), (down, down_send), (over, over_send)):
                @pl.when(way)
                def _():
                    whole_ket(f, sem).wait_send()
            return carry

        lax.fori_loop(1, STEPS, settle, 0)
        for d in COLUMN + [0]:
            send_table(d).wait_send()

        @pl.when(z == 0)
        def _():
            for d in COLUMN + [0]:
                send_first(d).wait_send()

        @pl.when(z > 0)
        def _():
            for d in COLUMN + [0]:
                send_bt(d).wait_send()

    @pl.when(core == 1)
    def _():
        prod[TRIP] = jnp.zeros((ROWS, TILE), F32)
        bt[site] = bt_out[z]
        pl.semaphore_wait(barrier, 1 + N_PLANE + 2 * N_COLUMN)
        own_ket.wait()
        for d in COLUMN:
            send_table(d).start()

        @pl.when(site < STEPS)
        def _():
            for q in range(PIECES):
                ket_piece(site, q, over_send, z * 2).start()

        def start_bt():
            for d in COLUMN:
                send_bt(d).start()

        @pl.when(site == 1)
        def _():
            start_bt()

        def send_part(p, i):
            return remote(
                part.at[p, i], got.at[p, i], part_send.at[p], part_recv.at[p], site, slot_at(PLANE[i])
            )

        def all_parts(p):
            span = pl.ds(0, N_PLANE)
            return remote(
                part.at[p, span], got.at[p, span], part_send.at[p], part_recv.at[p],
                site, slot_at(PLANE[0]),
            )

        def send_rows(q, d):
            held = env.at[q, rows]
            return remote(held, held, env_send.at[q], env_recv.at[q], plane_at(d) * 2 + 1)

        def all_rows(q):
            held = env.at[q, pl.ds(0, N_COLUMN * ROWS)]
            return remote(held, held, env_send.at[q], env_recv.at[q], plane_at(COLUMN[0]) * 2 + 1)

        def scatter(j, p):
            def summed(slot):
                return (prod[lookup[j, 0, slot]] + prod[lookup[j, 1, slot]]).astype(BF16)

            for i in range(N_PLANE):
                part[p, i] = summed(slot_at(PLANE[i]))
                send_part(p, i).start()
            got[p, N_PLANE] = summed(sector)

        def gather(p):
            all_parts(p).wait_recv()
            total = got[p, 0].astype(F32)
            for i in range(1, SLOTS):
                total += got[p, i].astype(F32)
            env[1 - p, rows] = total.astype(BF16)
            for d in COLUMN:
                send_rows(1 - p, d).start()

        arrived = tables.at[pl.ds(0, 2 * NZ - 1)]
        remote(arrived, arrived, table_send, table_recv, z * 2).wait_recv()
        fetch = pltpu.make_async_copy(tables, lookup, local_sem)
        fetch.start()
        remote(first_in, first_in, first_send, first_recv, z * 2).wait_recv()
        for k in range(TRIP):
            prod[k] = first_in[k * ROWS:(k + 1) * ROWS].astype(F32)
        fetch.wait()
        scatter(0, 0)

        @pl.when(site == 3)
        def _():
            start_bt()

        gather(0)

        def step(j, carry):
            p = lax.rem(j, 2)

            @pl.when(j != site)
            def _():
                remote(bt.at[j], bt.at[j], bt_send, bt_recv.at[j], z * 2).wait_recv()
                whole_ket(j, over_send).wait_recv()

            all_rows(p).wait_recv()
            left = jnp.dot(bt[j], env[p], preferred_element_type=F32).astype(BF16)
            for k in range(TRIP):
                prod[k] = jnp.dot(
                    left[k * ROWS:(k + 1) * ROWS], kets[j, k], preferred_element_type=F32
                )
            scatter(j, p)
            all_parts(1 - p).wait_send()
            all_rows(p).wait_send()

            @pl.when(j == z * 2)
            def _():
                leave[...] = env[p]
                to_core_0().start()

            @pl.when(j == site)
            def _():
                out_ref[...] = env[p]

            @pl.when((j == site - 3) & (site < STEPS))
            def _():
                start_bt()

            gather(p)
            return carry

        lax.fori_loop(1, STEPS, step, 0)
        last = STEPS % 2
        all_rows(last).wait_recv()

        @pl.when(site == STEPS)
        def _():
            out_ref[...] = env[last]

        all_rows(last).wait_send()
        all_parts(1 - last).wait_send()

        @pl.when(z > 0)
        def _():
            to_core_0().wait_send()

        @pl.when(site < STEPS)
        def _():
            whole_ket(site, over_send).wait_send()
            for d in COLUMN:
                send_bt(d).wait_send()

        for d in COLUMN:
            send_table(d).wait_send()


def run_chain(env, bra, ket, table, weight):
    vmem = pl.BlockSpec(memory_space=pltpu.VMEM)
    smem = pl.BlockSpec(memory_space=pltpu.SMEM)
    dma = pltpu.SemaphoreType.DMA
    return pl.pallas_call(
        chain,
        out_shape=jax.ShapeDtypeStruct((TILE, TILE), BF16),
        in_specs=[vmem, vmem, vmem, vmem, smem],
        out_specs=vmem,
        scratch_shapes=[
            pltpu.VMEM((2, TILE, TILE), BF16),
            pltpu.VMEM((TRIP + 1, ROWS, TILE), F32),
            pltpu.VMEM((2, N_PLANE, ROWS, TILE), BF16),
            pltpu.VMEM((2, SLOTS, ROWS, TILE), BF16),
            pltpu.VMEM((TILE, TILE), BF16),
            pltpu.VMEM((TILE, TILE), BF16),
            pltpu.VMEM((NZ, TRIP * ROWS, TILE), BF16),
            pltpu.VMEM((2 * NZ, TRIP * ROWS, TILE), BF16),
            pltpu.VMEM((NZ, TRIP * ROWS, TILE), BF16),
            pltpu.VMEM((TRIP * ROWS, TILE), BF16),
            pltpu.VMEM((2 * NZ, TRIP, TILE, TILE), BF16),
            pltpu.VMEM((2 * NZ, 8, TILE), jnp.int32),
            pltpu.SMEM((2 * NZ, 8, TILE), jnp.int32),
            dma((2,)), dma((2,)), dma((2,)), dma((2,)), dma, dma, dma, dma((2 * NZ,)),
            dma, dma, dma, dma, dma,
            dma, dma, dma, dma((2 * NZ, PIECES)),
        ],
        compiler_params=pltpu.CompilerParams(
            collective_id=0, has_side_effects=True, vmem_limit_bytes=40 << 20
        ),
        name="chain",
    )(env, bra, ket, table, weight)


def lookups(joining_out, joining_mpo, owner, mpo_weight):
    slots = jnp.arange(SLOTS, dtype=jnp.int32)
    outputs = joining_out[0, :, 0]
    target = jnp.sum(jnp.where(outputs[:, None] == slots[None, :], owner[None, :], 0), axis=1)
    terms = jnp.arange(mpo_weight.shape[1], dtype=jnp.int32)
    weights = jnp.sum(
        jnp.where(joining_mpo[0][:, None] == terms[None, :], mpo_weight[0][None, :], 0.0), axis=1
    )
    place = jnp.arange(TRIP, dtype=jnp.int32)[:, None]
    hit = target[:, None] == slots[None, :]
    first = jnp.min(jnp.where(hit, place, TRIP), axis=0)
    second = jnp.min(jnp.where(hit & (place != first[None, :]), place, TRIP), axis=0)
    return first, second, weights


def local(left_env, mps_bra, mps_ket, joining_out, joining_mpo, owner, mpo_weight):
    first, second, weights = lookups(joining_out, joining_mpo, owner, mpo_weight)
    table = jnp.pad(jnp.stack([first, second]), ((0, 6), (0, TILE - SLOTS)))
    return run_chain(left_env[0], mps_bra[0], mps_ket[0], table, weights)[None, None]


def solution(mesh):
    return jax.shard_map(
        local,
        mesh=mesh,
        in_specs=(
            P("sector", None, None),
            P("site", "sector", None, None),
            P("site", "sector", None, None),
            P("site", "sector", None),
            P("site", "sector"),
            P(),
            P("site", None),
        ),
        out_specs=P("site", "sector", None, None),
        check_vma=False,
    )
```

time: 247 us -> 194 us (0.79)
  blocking collectives: 62.7 us -> 0 us
  Pallas kernels: 146 us -> 188 us
  between operations: 14.7 us -> 0.04 us
  starting transfers between devices: 11.8 us -> 0 us
  local copies, waits for them, and re-layouts: 9.18 us -> 4.77 us
    unnamed x2 -> x0, blocking collectives: 62.7 us -> none
    pallas_call x1, Pallas kernels: 146 us -> 188 us  [run_chain(): pl.pallas_call(chain, out_shape=jax.ShapeDtypeStruct((TILE, TILE), BF16),...]
    all_to_all x1 -> x0, starting transfers between devices: 11.8 us -> none  [local(): bt = lax.all_to_all(bt, 'site', split_axis=0, concat_axis=0, tiled=True)]
    unnamed x10 -> x15, local copies, waits for them, and re-layouts: 7.57 us -> 4.76 us
  transfers between devices with their start and end apart: 2 -> 0, of which waited for: 1 -> 0; matrix products, arithmetic and copies ran while one was open for 3% -> 0% of each run, Pallas kernels for 0% -> 0%
where the time goes in v2:
time: 194 us
  Pallas kernels  188 us (97%)
  local copies, waits for them, and re-layouts  4.77 us (2%)
    pallas_call x1, Pallas kernels, run_chain(): pl.pallas_call(chain, out_shape=jax.ShapeDtypeStruct((TILE, TILE), BF16),...  188 us
    unnamed x15, local copies, waits for them, and re-layouts  4.76 us

profile of v2, /device:TPU:1, one launch (start us, length us, event | category | flops | bytes accessed | tf_op | source)
XLA Modules:
  0.0 193.6 jit_solution(7063203068918606809)
XLA Ops:
  0.0 0.0 copy-start.3
  0.0 0.0 copy-start.4
  0.0 0.7 copy-done.3
  0.7 0.0 copy-done.4
  0.7 0.2 select_reduce_fusion.2
  0.9 0.1 select_reduce_fusion.1
  0.9 0.1 select_reduce_fusion
  1.0 0.0 copy-start.5
  1.0 0.0 copy-start.6
  1.1 0.6 copy-done.5
  1.7 0.0 copy-done.6
  1.7 0.1 select_reduce_fusion.3.weight_ref
  1.8 0.0 copy-start
  1.8 1.0 copy-done
  2.8 0.0 copy-start.1
  2.8 1.0 copy-done.1
  3.9 0.0 copy-start.2
  3.9 0.8 copy-done.2
  4.6 188.3 %chain.1 = bf16[128,128]{1,0:T(8,128)(2,1)S(1)} custom-call(bf16[128,128]{1,0:T(8,128)(2,1)S(1)} %bitcast.12, bf16[16,128,128]{2,1,0:T(8,128)(2,1)S(1)} %bitcast.9, bf16[16,128,128]{2,1,0:T(8,128)(2,1)S(1)} %bitcast.10, s32[8,128]{1,0:T(8,128)S(1)} %pad.4.table_ref, f32[16]{0:T(128)S(1)} %select_reduce_fusion.3.weight_ref), custom_call_target="tpu_custom_call" | custom-call | tf_op jit(solution)/shard_map/chain/pallas_call | solution.py:338
  193.0 0.6 copy.9
  (2 shorter events, 0.0 us)
Async XLA Ops:
  0.0 0.7 copy-start.3
  0.0 0.7 copy-start.4
  1.0 0.7 copy-start.5
  1.0 0.7 copy-start.6
  1.8 1.0 copy-start
  2.8 1.0 copy-start.1
  3.9 0.8 copy-start.2

commit v3 on v2

v3 whole, which is shorter than its diff:
```python
import functools

import jax
import jax.numpy as jnp
from jax import lax
from jax.experimental import pallas as pl
from jax.experimental.pallas import tpu as pltpu
from jax.sharding import PartitionSpec as P

MESH = pl.DeviceIdType.MESH
BF16 = jnp.bfloat16
F32 = jnp.float32

NX, NY, NZ = 4, 8, 8
SLOTS = NX * NY
STEPS = 15
TRIP = 16
ROWS = 16
TILE = 128
PIECES = 16
PIECE = TRIP // PIECES


def hops(offset):
    dy, dx = offset
    return min(dy, NY - dy) + min(dx, NX - dx)


PLANE = sorted(
    [(dy, dx) for dy in range(NY) for dx in range(NX) if (dy, dx) != (0, 0)], key=hops, reverse=True
)
COLUMN = sorted(range(1, NZ), key=lambda d: min(d, NZ - d), reverse=True)
N_PLANE = len(PLANE)
N_COLUMN = len(COLUMN)


def chain(
    env_ref, bra_ref, ket_ref, outputs_ref, terms_ref, owner_ref, weight_ref, out_ref,
    bra, env, prod, part, got, leave, land, bt_out, bt, first_out, first_in, kets, tables, lookup,
    part_send, part_recv, env_send, env_recv, out_send, out_recv, bt_send, bt_recv,
    first_send, first_recv, table_send, table_recv, table_sem, local_sem,
    up_send, down_send, over_send, ket_recv,
):
    site = lax.axis_index("site")
    sector = lax.axis_index("sector")
    z, core = site // 2, lax.rem(site, 2)
    y, x = sector // NX, lax.rem(sector, NX)
    rows = pl.ds(pl.multiple_of(z * ROWS, ROWS), ROWS)

    def slot_at(offset):
        return lax.rem(y + offset[0], NY) * NX + lax.rem(x + offset[1], NX)

    def plane_at(d):
        return lax.rem(z + d, NZ)

    def remote(src, dst, send_sem, recv_sem, to_site, to_sector=sector):
        return pltpu.make_async_remote_copy(
            src_ref=src, dst_ref=dst, send_sem=send_sem, recv_sem=recv_sem,
            device_id=(to_site, to_sector), device_id_type=MESH,
        )

    barrier = pltpu.get_barrier_semaphore()

    def greet(to_site, to_sector=sector):
        pl.semaphore_signal(barrier, inc=1, device_id=(to_site, to_sector), device_id_type=MESH)

    def send_table(d):
        return remote(tables.at[site], tables.at[site], table_send, table_recv.at[site], plane_at(d) * 2 + 1)

    def send_bt(d):
        return remote(
            bt_out.at[plane_at(d)], bt.at[site], bt_send, bt_recv.at[site], plane_at(d) * 2 + 1
        )

    def send_first(d):
        return remote(
            first_out.at[plane_at(d)], first_in, first_send, first_recv, plane_at(d) * 2 + 1
        )

    def to_core_0():
        return remote(leave, land, out_send, out_recv, z * 2)

    def ket_piece(f, q, send_sem, to_site):
        held = kets.at[f, pl.ds(q * PIECE, PIECE)]
        return remote(held, held, send_sem, ket_recv.at[f, q], to_site)

    def whole_ket(f, send_sem, tiles=TRIP):
        held = kets.at[f, pl.ds(0, tiles)]
        return remote(held, held, send_sem, ket_recv.at[f, 0], site + 1 - 2 * core)

    own_ket = pltpu.make_async_copy(ket_ref, kets.at[site], local_sem.at[0])
    own_bra = pltpu.make_async_copy(bra_ref, bra, local_sem.at[1])
    own_ket.start()
    own_bra.start()
    @pl.when(core == 0)
    def _():
        greet(plane_at(1) * 2)
        greet(plane_at(NZ - 1) * 2)

        @pl.when(z > 0)
        def _():
            greet(site + 1)

        @pl.when((z == 1) | (z == NZ - 1))
        def _():
            greet(1)

    @pl.when(core == 1)
    def _():
        for offset in PLANE:
            greet(site, slot_at(offset))
        for d in COLUMN:
            greet(plane_at(d) * 2 + 1)
            greet(plane_at(d) * 2)
        greet(site - 1)

    lane = lax.broadcasted_iota(jnp.int32, (8, TILE), 1)
    first = jnp.full((8, TILE), TRIP, jnp.int32)
    second = first
    for k in reversed(range(TRIP)):
        hit = lane == owner_ref[outputs_ref[k]]
        second = jnp.where(hit, first, second)
        first = jnp.where(hit, k, first)
    upper = lax.broadcasted_iota(jnp.int32, (8, TILE), 0) == 0
    tables[site] = jnp.where(upper, first, second)

    own_bra.wait()
    for k in range(TRIP):
        turned = jnp.transpose(bra[k].astype(F32)) * weight_ref[terms_ref[k]]
        bt_out[:, k * ROWS:(k + 1) * ROWS, :] = turned.astype(BF16).reshape(NZ, ROWS, TILE)
    own_ket.wait()

    @pl.when(core == 0)
    def _():
        pl.semaphore_wait(barrier, N_COLUMN + 3)

        @pl.when(z == 0)
        def _():
            def chunk(i, carry):
                d = NZ // 2 + (1 - 2 * lax.rem(i, 2)) * ((i + 1) // 2)
                to = plane_at(d)
                left = jnp.dot(bt_out[to], env_ref[...], preferred_element_type=F32).astype(BF16)
                for k in range(TRIP):
                    span = pl.ds(k * ROWS, ROWS)
                    value = jnp.dot(
                        left[k * ROWS:(k + 1) * ROWS], kets[0, k], preferred_element_type=F32
                    )
                    first_out[to, span] = value.astype(BF16)
                send_table(d).start()
                send_first(d).start()
                return carry

            lax.fori_loop(0, NZ, chunk, 0)
            out_ref[...] = env_ref[...]

        @pl.when(z > 0)
        def _():
            for d in COLUMN + [0]:
                send_table(d).start()

        @pl.when(z > 0)
        def _():
            for q in range(PIECES):
                ket_piece(site, q, up_send, plane_at(1) * 2).start()
                ket_piece(site, q, down_send, plane_at(NZ - 1) * 2).start()
                held = kets.at[site, pl.ds(q * PIECE, PIECE)]
                remote(held, held, over_send, ket_recv.at[site, 0], z * 2 + 1).start()

        def serve(f, carry):
            away = lax.rem(z - f // 2 + NZ, NZ)

            @pl.when(f == site)
            def _():
                for d in COLUMN + [0]:
                    send_bt(d).start()

            @pl.when((f != site) & ((f != 1) | (z != 0)))
            def _():
                for q in range(PIECES):
                    ket_piece(f, q, up_send, z * 2 + 1).wait_recv()
                    if 2 * q < PIECES:
                        up, down = away < NZ // 2, (away == 0) | (away > NZ // 2 + 1)
                    else:
                        up, down = away < NZ // 2 - 1, (away == 0) | (away > NZ // 2)
                    held = kets.at[f, pl.ds(q * PIECE, PIECE)]

                    @pl.when(up)
                    def _():
                        ket_piece(f, q, up_send, plane_at(1) * 2).start()

                    @pl.when(down)
                    def _():
                        ket_piece(f, q, down_send, plane_at(NZ - 1) * 2).start()

                    @pl.when(away > 0)
                    def _():
                        remote(held, held, over_send, ket_recv.at[f, 0], z * 2 + 1).start()

            return carry

        lax.fori_loop(1, STEPS, serve, 0)

        @pl.when(z > 0)
        def _():
            to_core_0().wait_recv()
            out_ref[...] = land[...]

        def settle(f, carry):
            away = lax.rem(z - f // 2 + NZ, NZ)
            live = (f != 1) | (z != 0)

            @pl.when(live & (away < NZ // 2 - 1))
            def _():
                whole_ket(f, up_send).wait_send()

            @pl.when(live & (away == NZ // 2 - 1))
            def _():
                whole_ket(f, up_send, TRIP // 2).wait_send()

            @pl.when(live & ((away == 0) | (away > NZ // 2 + 1)))
            def _():
                whole_ket(f, down_send).wait_send()

            @pl.when(live & (away == NZ // 2 + 1))
            def _():
                whole_ket(f, down_send, TRIP // 2).wait_send()

            @pl.when((away > 0) | (f == site))
            def _():
                whole_ket(f, over_send).wait_send()

            return carry

        lax.fori_loop(1, STEPS, settle, 0)
        for d in COLUMN + [0]:
            send_table(d).wait_send()

        @pl.when(z == 0)
        def _():
            for d in COLUMN + [0]:
                send_first(d).wait_send()

        @pl.when(z > 0)
        def _():
            for d in COLUMN + [0]:
                send_bt(d).wait_send()

    @pl.when(core == 1)
    def _():
        prod[TRIP] = jnp.zeros((ROWS, TILE), F32)
        bt[site] = bt_out[z]
        pl.semaphore_wait(barrier, N_PLANE + N_COLUMN + jnp.where(z == 0, 2, 1))
        @pl.when(site < STEPS)
        def _():
            for d in COLUMN:
                send_table(d).start()

        @pl.when((site > 1) & (site < STEPS))
        def _():
            for q in range(PIECES):
                ket_piece(site, q, over_send, z * 2).start()

        def start_bt():
            for d in COLUMN:
                send_bt(d).start()

        @pl.when(site == 1)
        def _():
            for q in range(PIECES):
                ket_piece(1, q, up_send, plane_at(1) * 2).start()
                ket_piece(1, q, down_send, plane_at(NZ - 1) * 2).start()
            start_bt()

        def send_part(p, i):
            return remote(
                part.at[p, i], got.at[p, i], part_send.at[p], part_recv.at[p], site, slot_at(PLANE[i])
            )

        def all_parts(p):
            span = pl.ds(0, N_PLANE)
            return remote(
                part.at[p, span], got.at[p, span], part_send.at[p], part_recv.at[p],
                site, slot_at(PLANE[0]),
            )

        def send_rows(q, d):
            held = env.at[q, rows]
            return remote(held, held, env_send.at[q], env_recv.at[q], plane_at(d) * 2 + 1)

        def all_rows(q):
            held = env.at[q, pl.ds(0, N_COLUMN * ROWS)]
            return remote(held, held, env_send.at[q], env_recv.at[q], plane_at(COLUMN[0]) * 2 + 1)

        def scatter(p):
            def summed(slot):
                return (prod[lookup[p, 0, slot]] + prod[lookup[p, 1, slot]]).astype(BF16)

            for i in range(N_PLANE):
                part[p, i] = summed(slot_at(PLANE[i]))
                send_part(p, i).start()
            got[p, N_PLANE] = summed(sector)

        def gather(p):
            all_parts(p).wait_recv()
            total = got[p, 0].astype(F32)
            for i in range(1, SLOTS):
                total += got[p, i].astype(F32)
            env[1 - p, rows] = total.astype(BF16)
            for d in COLUMN:
                send_rows(1 - p, d).start()

        def fetch(j, p):
            return pltpu.make_async_copy(tables.at[j], lookup.at[p], table_sem.at[p])

        def fetch_table(j, p):
            @pl.when(j != site)
            def _():
                remote(tables.at[j], tables.at[j], table_send, table_recv.at[j], z * 2).wait_recv()

            fetch(j, p).start()

        fetch_table(0, 0)
        remote(first_in, first_in, first_send, first_recv, z * 2).wait_recv()
        for k in range(TRIP):
            prod[k] = first_in[k * ROWS:(k + 1) * ROWS].astype(F32)
        fetch(0, 0).wait()
        scatter(0)
        fetch_table(1, 1)

        @pl.when(site == 3)
        def _():
            start_bt()

        gather(0)

        def step(j, carry):
            p = lax.rem(j, 2)

            @pl.when(j != site)
            def _():
                remote(bt.at[j], bt.at[j], bt_send, bt_recv.at[j], z * 2).wait_recv()
                whole_ket(j, over_send).wait_recv()

            all_rows(p).wait_recv()
            left = jnp.dot(bt[j], env[p], preferred_element_type=F32).astype(BF16)
            for k in range(TRIP):
                prod[k] = jnp.dot(
                    left[k * ROWS:(k + 1) * ROWS], kets[j, k], preferred_element_type=F32
                )
            fetch(j, p).wait()
            scatter(p)

            @pl.when(j < STEPS - 1)
            def _():
                fetch_table(j + 1, 1 - p)

            all_parts(1 - p).wait_send()
            all_rows(p).wait_send()

            @pl.when(j == z * 2)
            def _():
                leave[...] = env[p]
                to_core_0().start()

            @pl.when(j == site)
            def _():
                out_ref[...] = env[p]

            @pl.when((j == site - 3) & (site < STEPS))
            def _():
                start_bt()

            gather(p)
            return carry

        lax.fori_loop(1, STEPS, step, 0)
        last = STEPS % 2
        all_rows(last).wait_recv()

        @pl.when(site == STEPS)
        def _():
            out_ref[...] = env[last]

        all_rows(last).wait_send()
        all_parts(1 - last).wait_send()

        @pl.when(z > 0)
        def _():
            to_core_0().wait_send()

        @pl.when(site < STEPS)
        def _():
            for d in COLUMN:
                send_table(d).wait_send()
                send_bt(d).wait_send()

        @pl.when((site > 1) & (site < STEPS))
        def _():
            whole_ket(site, over_send).wait_send()

        @pl.when(site == 1)
        def _():
            whole_ket(1, up_send).wait_send()
            whole_ket(1, down_send).wait_send()


def run_chain(env, bra, ket, outputs, terms, owner, weight):
    vmem = pl.BlockSpec(memory_space=pltpu.VMEM)
    smem = pl.BlockSpec(memory_space=pltpu.SMEM)
    anywhere = pl.BlockSpec(memory_space=pl.ANY)
    dma = pltpu.SemaphoreType.DMA
    return pl.pallas_call(
        chain,
        out_shape=jax.ShapeDtypeStruct((TILE, TILE), BF16),
        in_specs=[vmem, anywhere, anywhere, smem, smem, smem, smem],
        out_specs=vmem,
        scratch_shapes=[
            pltpu.VMEM((TRIP, TILE, TILE), BF16),
            pltpu.VMEM((2, TILE, TILE), BF16),
            pltpu.VMEM((TRIP + 1, ROWS, TILE), F32),
            pltpu.VMEM((2, N_PLANE, ROWS, TILE), BF16),
            pltpu.VMEM((2, SLOTS, ROWS, TILE), BF16),
            pltpu.VMEM((TILE, TILE), BF16),
            pltpu.VMEM((TILE, TILE), BF16),
            pltpu.VMEM((NZ, TRIP * ROWS, TILE), BF16),
            pltpu.VMEM((2 * NZ, TRIP * ROWS, TILE), BF16),
            pltpu.VMEM((NZ, TRIP * ROWS, TILE), BF16),
            pltpu.VMEM((TRIP * ROWS, TILE), BF16),
            pltpu.VMEM((2 * NZ, TRIP, TILE, TILE), BF16),
            pltpu.VMEM((2 * NZ, 8, TILE), jnp.int32),
            pltpu.SMEM((2, 8, TILE), jnp.int32),
            dma((2,)), dma((2,)), dma((2,)), dma((2,)), dma, dma, dma, dma((2 * NZ,)),
            dma, dma, dma, dma((2 * NZ,)), dma((2,)), dma((2,)),
            dma, dma, dma, dma((2 * NZ, PIECES)),
        ],
        compiler_params=pltpu.CompilerParams(
            collective_id=0, has_side_effects=True, vmem_limit_bytes=56 << 20
        ),
        name="chain",
    )(env, bra, ket, outputs, terms, owner, weight)


def local(left_env, mps_bra, mps_ket, joining_out, joining_mpo, owner, mpo_weight):
    envs = run_chain(
        left_env[0], mps_bra[0], mps_ket[0], joining_out[0, :, 0], joining_mpo[0], owner, mpo_weight[0]
    )
    return envs[None, None]


def solution(mesh):
    return jax.shard_map(
        local,
        mesh=mesh,
        in_specs=(
            P("sector", None, None),
            P("site", "sector", None, None),
            P("site", "sector", None, None),
            P("site", "sector", None),
            P("site", "sector"),
            P(),
            P("site", None),
        ),
        out_specs=P("site", "sector", None, None),
        check_vma=False,
    )
```

time: 194 us -> 180 us (0.928)
  Pallas kernels: 188 us -> 178 us
  local copies, waits for them, and re-layouts: 4.77 us -> 1.38 us
    pallas_call x1, Pallas kernels: 188 us -> 178 us  [run_chain(): pl.pallas_call(chain, out_shape=jax.ShapeDtypeStruct((TILE, TILE), BF16),...]
    unnamed x15 -> x1, local copies, waits for them, and re-layouts: 4.76 us -> 1.38 us
where the time goes in v3:
time: 180 us; the launch traced here: 179 us
  Pallas kernels  178 us (99%)
    pallas_call x1, Pallas kernels, run_chain(): pl.pallas_call(chain, out_shape=jax.ShapeDtypeStruct((TILE, TILE), BF16),...  178 us

profile of v3, /device:TPU:1, one launch (start us, length us, event | category | flops | bytes accessed | tf_op | source)
XLA Modules:
  0.0 179.5 jit_solution(6823707337996560742)
XLA Ops:
  0.0 178.1 %chain.1 = bf16[128,128]{1,0:T(8,128)(2,1)} custom-call(bf16[128,128]{1,0:T(8,128)(2,1)} %bitcast.10, bf16[16,128,128]{2,1,0:T(8,128)(2,1)} %bitcast.7, bf16[16,128,128]{2,1,0:T(8,128)(2,1)} %bitcast.8, s32[16]{0:T(128)} %bitcast.11, s32[16]{0:T(128)} %bitcast.12, s32[32]{0:T(128)} %owner_ref.1, f32[8]{0:T(128)} %bitcast.13), custom_call_target="tpu_custom_call" | custom-call | tf_op jit(solution)/shard_map/chain/pallas_call | solution.py:412
  178.1 1.4 copy.9

commit v4 on v3

--- a/solution.py
+++ b/solution.py
@@ -19,6 +19,7 @@
 TILE = 128
 PIECES = 16
 PIECE = TRIP // PIECES
+LEAD = 8
 
 
 def hops(offset):
@@ -32,6 +33,7 @@
 COLUMN = sorted(range(1, NZ), key=lambda d: min(d, NZ - d), reverse=True)
 N_PLANE = len(PLANE)
 N_COLUMN = len(COLUMN)
+N_FAR = sum(hops(offset) > 4 for offset in PLANE)
 
 
 def chain(
@@ -39,7 +41,7 @@
     bra, env, prod, part, got, leave, land, bt_out, bt, first_out, first_in, kets, tables, lookup,
     part_send, part_recv, env_send, env_recv, out_send, out_recv, bt_send, bt_recv,
     first_send, first_recv, table_send, table_recv, table_sem, local_sem,
-    up_send, down_send, over_send, ket_recv,
+    up_send, down_send, over_send, ket_recv, gate,
 ):
     site = lax.axis_index("site")
     sector = lax.axis_index("sector")
@@ -72,10 +74,9 @@
             bt_out.at[plane_at(d)], bt.at[site], bt_send, bt_recv.at[site], plane_at(d) * 2 + 1
         )
 
-    def send_first(d):
-        return remote(
-            first_out.at[plane_at(d)], first_in, first_send, first_recv, plane_at(d) * 2 + 1
-        )
+    def send_first(c, i):
+        to_sector = sector if i == N_PLANE else slot_at(PLANE[i])
+        return remote(first_out.at[c, i], first_in.at[c, i], first_send, first_recv.at[c], 1, to_sector)
 
     def to_core_0():
         return remote(leave, land, out_send, out_recv, z * 2)
@@ -92,6 +93,19 @@
     own_bra = pltpu.make_async_copy(bra_ref, bra, local_sem.at[1])
     own_ket.start()
     own_bra.start()
+    def fetch(j, p):
+        return pltpu.make_async_copy(tables.at[j], lookup.at[p], table_sem.at[p])
+
+    def products(bt_chunk, block, j):
+        left = jnp.dot(bt_chunk, block, preferred_element_type=F32).astype(BF16)
+        for k in range(TRIP):
+            prod[k] = jnp.dot(
+                left[k * ROWS:(k + 1) * ROWS], kets[j, k], preferred_element_type=F32
+            )
+
+    def summed(p, slot):
+        return (prod[lookup[p, 0, slot]] + prod[lookup[p, 1, slot]]).astype(BF16)
+
     @pl.when(core == 0)
     def _():
         greet(plane_at(1) * 2)
@@ -101,14 +115,14 @@
         def _():
             greet(site + 1)
 
-        @pl.when((z == 1) | (z == NZ - 1))
-        def _():
-            greet(1)
-
     @pl.when(core == 1)
     def _():
         for offset in PLANE:
             greet(site, slot_at(offset))
+
+            @pl.when(z == 0)
+            def _():
+                greet(0, slot_at(offset))
         for d in COLUMN:
             greet(plane_at(d) * 2 + 1)
             greet(plane_at(d) * 2)
@@ -132,22 +146,19 @@
 
     @pl.when(core == 0)
     def _():
-        pl.semaphore_wait(barrier, N_COLUMN + 3)
+        pl.semaphore_wait(barrier, N_COLUMN + 3 + jnp.where(z == 0, N_PLANE, 0))
 
         @pl.when(z == 0)
         def _():
-            def chunk(i, carry):
-                d = NZ // 2 + (1 - 2 * lax.rem(i, 2)) * ((i + 1) // 2)
-                to = plane_at(d)
-                left = jnp.dot(bt_out[to], env_ref[...], preferred_element_type=F32).astype(BF16)
-                for k in range(TRIP):
-                    span = pl.ds(k * ROWS, ROWS)
-                    value = jnp.dot(
-                        left[k * ROWS:(k + 1) * ROWS], kets[0, k], preferred_element_type=F32
-                    )
-                    first_out[to, span] = value.astype(BF16)
-                send_table(d).start()
-                send_first(d).start()
+            prod[TRIP] = jnp.zeros((ROWS, TILE), F32)
+            fetch(0, 0).start()
+            fetch(0, 0).wait()
+
+            def chunk(c, carry):
+                products(bt_out[c], env_ref[...], 0)
+                for i in range(SLOTS):
+                    first_out[c, i] = summed(0, sector if i == N_PLANE else slot_at(PLANE[i]))
+                    send_first(c, i).start()
                 return carry
 
             lax.fori_loop(0, NZ, chunk, 0)
@@ -158,23 +169,37 @@
             for d in COLUMN + [0]:
                 send_table(d).start()
 
-        @pl.when(z > 0)
-        def _():
+        def send_own(up, down):
             for q in range(PIECES):
-                ket_piece(site, q, up_send, plane_at(1) * 2).start()
-                ket_piece(site, q, down_send, plane_at(NZ - 1) * 2).start()
-                held = kets.at[site, pl.ds(q * PIECE, PIECE)]
-                remote(held, held, over_send, ket_recv.at[site, 0], z * 2 + 1).start()
+                if up:
+                    ket_piece(site, q, up_send, plane_at(1) * 2).start()
+                if down:
+                    held = kets.at[site, pl.ds(q * PIECE, PIECE)]
+                    ket_piece(site, q, down_send, plane_at(NZ - 1) * 2).start()
+                    remote(held, held, over_send, ket_recv.at[site, 0], z * 2 + 1).start()
+
+        @pl.when(z == 1)
+        def _():
+            send_own(False, True)
+
+        @pl.when(z > 0)
+        def _():
+            pl.semaphore_wait(gate, 1)
+
+        @pl.when(z == 1)
+        def _():
+            send_own(True, False)
+
+        @pl.when(z > 0)
+        def _():
+            for d in COLUMN + [0]:
+                send_bt(d).start()
 
         def serve(f, carry):
             away = lax.rem(z - f // 2 + NZ, NZ)
 
-            @pl.when(f == site)
-            def _():
-                for d in COLUMN + [0]:
-                    send_bt(d).start()
-
-            @pl.when((f != site) & ((f != 1) | (z != 0)))
+
+            @pl.when(f != site)
             def _():
                 for q in range(PIECES):
                     ket_piece(f, q, up_send, z * 2 + 1).wait_recv()
@@ -196,9 +221,13 @@
                     def _():
                         remote(held, held, over_send, ket_recv.at[f, 0], z * 2 + 1).start()
 
+            @pl.when((f == jnp.minimum(site - 1, LEAD)) & (z > 1))
+            def _():
+                send_own(True, True)
+
             return carry
 
-        lax.fori_loop(1, STEPS, serve, 0)
+        lax.fori_loop(2, STEPS, serve, 0)
 
         @pl.when(z > 0)
         def _():
@@ -207,21 +236,20 @@
 
         def settle(f, carry):
             away = lax.rem(z - f // 2 + NZ, NZ)
-            live = (f != 1) | (z != 0)
-
-            @pl.when(live & (away < NZ // 2 - 1))
+
+            @pl.when(away < NZ // 2 - 1)
             def _():
                 whole_ket(f, up_send).wait_send()
 
-            @pl.when(live & (away == NZ // 2 - 1))
+            @pl.when(away == NZ // 2 - 1)
             def _():
                 whole_ket(f, up_send, TRIP // 2).wait_send()
 
-            @pl.when(live & ((away == 0) | (away > NZ // 2 + 1)))
+            @pl.when((away == 0) | (away > NZ // 2 + 1))
             def _():
                 whole_ket(f, down_send).wait_send()
 
-            @pl.when(live & (away == NZ // 2 + 1))
+            @pl.when(away == NZ // 2 + 1)
             def _():
                 whole_ket(f, down_send, TRIP // 2).wait_send()
 
@@ -231,25 +259,22 @@
 
             return carry
 
-        lax.fori_loop(1, STEPS, settle, 0)
-        for d in COLUMN + [0]:
-            send_table(d).wait_send()
-
+        lax.fori_loop(2, STEPS, settle, 0)
         @pl.when(z == 0)
         def _():
+            remote(first_out, first_in, first_send, first_recv.at[0], 1).wait_send()
+
+        @pl.when(z > 0)
+        def _():
             for d in COLUMN + [0]:
-                send_first(d).wait_send()
-
-        @pl.when(z > 0)
-        def _():
-            for d in COLUMN + [0]:
+                send_table(d).wait_send()
                 send_bt(d).wait_send()
 
     @pl.when(core == 1)
     def _():
         prod[TRIP] = jnp.zeros((ROWS, TILE), F32)
         bt[site] = bt_out[z]
-        pl.semaphore_wait(barrier, N_PLANE + N_COLUMN + jnp.where(z == 0, 2, 1))
+        pl.semaphore_wait(barrier, N_PLANE + N_COLUMN + jnp.where(z == 0, 0, 1))
         @pl.when(site < STEPS)
         def _():
             for d in COLUMN:
@@ -264,22 +289,53 @@
             for d in COLUMN:
                 send_bt(d).start()
 
+        half = PIECES // 2
+
+        def first_kets(pieces, up, down, source=False):
+            for q in pieces:
+                for way, sem, d in ((up, up_send, 1), (down, down_send, NZ - 1)):
+                    @pl.when(way)
+                    def _():
+                        if not source:
+                            ket_piece(1, q, sem, site).wait_recv()
+                        ket_piece(1, q, sem, plane_at(d) * 2 + 1).start()
+
+        def take_kets(pieces):
+            for q in pieces:
+                ket_piece(1, q, up_send, site).wait_recv()
+
+        first_kets(range(PIECES), z == 0, z == 0, source=True)
+
         @pl.when(site == 1)
         def _():
-            for q in range(PIECES):
-                ket_piece(1, q, up_send, plane_at(1) * 2).start()
-                ket_piece(1, q, down_send, plane_at(NZ - 1) * 2).start()
             start_bt()
+
+        next_up, next_down = (z == 1) | (z == 2), (z == NZ - 1) | (z == NZ - 2)
+        first_kets(range(half), next_up | (z == 3), next_down)
+        first_kets(range(half, PIECES), next_up, next_down | (z == NZ - 3))
+
+        @pl.when(z > 0)
+        def _():
+            pl.semaphore_signal(gate, inc=1, device_id=(z * 2, sector), device_id_type=MESH)
+
+        @pl.when((z == 4) | (z == 5))
+        def _():
+            take_kets(range(half))
+
+        @pl.when((z == 3) | (z == 4))
+        def _():
+            take_kets(range(half, PIECES))
 
         def send_part(p, i):
             return remote(
-                part.at[p, i], got.at[p, i], part_send.at[p], part_recv.at[p], site, slot_at(PLANE[i])
+                part.at[p, i], got.at[p, i], part_send.at[p], part_recv.at[p, int(i >= N_FAR)],
+                site, slot_at(PLANE[i]),
             )
 
-        def all_parts(p):
-            span = pl.ds(0, N_PLANE)
+        def some_parts(p, start, count, group=0):
+            span = pl.ds(start, count)
             return remote(
-                part.at[p, span], got.at[p, span], part_send.at[p], part_recv.at[p],
+                part.at[p, span], got.at[p, span], part_send.at[p], part_recv.at[p, group],
                 site, slot_at(PLANE[0]),
             )
 
@@ -292,26 +348,23 @@
             return remote(held, held, env_send.at[q], env_recv.at[q], plane_at(COLUMN[0]) * 2 + 1)
 
         def scatter(p):
-            def summed(slot):
-                return (prod[lookup[p, 0, slot]] + prod[lookup[p, 1, slot]]).astype(BF16)
-
             for i in range(N_PLANE):
-                part[p, i] = summed(slot_at(PLANE[i]))
+                part[p, i] = summed(p, slot_at(PLANE[i]))
                 send_part(p, i).start()
-            got[p, N_PLANE] = summed(sector)
+            got[p, N_PLANE] = summed(p, sector)
 
         def gather(p):
-            all_parts(p).wait_recv()
-            total = got[p, 0].astype(F32)
-            for i in range(1, SLOTS):
+            some_parts(p, N_FAR, N_PLANE - N_FAR, 1).wait_recv()
+            total = got[p, N_FAR].astype(F32)
+            for i in range(N_FAR + 1, SLOTS):
+                total += got[p, i].astype(F32)
+            some_parts(p, 0, N_FAR).wait_recv()
+            for i in range(N_FAR):
                 total += got[p, i].astype(F32)
             env[1 - p, rows] = total.astype(BF16)
             for d in COLUMN:
                 send_rows(1 - p, d).start()
 
-        def fetch(j, p):
-            return pltpu.make_async_copy(tables.at[j], lookup.at[p], table_sem.at[p])
-
         def fetch_table(j, p):
             @pl.when(j != site)
             def _():
@@ -319,19 +372,30 @@
 
             fetch(j, p).start()
 
-        fetch_table(0, 0)
-        remote(first_in, first_in, first_send, first_recv, z * 2).wait_recv()
-        for k in range(TRIP):
-            prod[k] = first_in[k * ROWS:(k + 1) * ROWS].astype(F32)
-        fetch(0, 0).wait()
-        scatter(0)
         fetch_table(1, 1)
 
-        @pl.when(site == 3)
-        def _():
-            start_bt()
-
-        gather(0)
+        @pl.when(z == 0)
+        def _():
+            def chunk(c, carry):
+                remote(first_in.at[c], first_in.at[c], first_send, first_recv.at[c], 0).wait_recv()
+                total = first_in[c, 0].astype(F32)
+                for i in range(1, SLOTS):
+                    total += first_in[c, i].astype(F32)
+                part_rows = pl.ds(pl.multiple_of(c * ROWS, ROWS), ROWS)
+                env[1, part_rows] = total.astype(BF16)
+                for d in COLUMN:
+                    held = env.at[1, part_rows]
+                    remote(held, held, env_send.at[1], env_recv.at[1], plane_at(d) * 2 + 1).start()
+                return carry
+
+            lax.fori_loop(0, NZ, chunk, 0)
+
+        def whole_env(q):
+            return remote(env.at[q], env.at[q], env_send.at[q], env_recv.at[q], plane_at(1) * 2 + 1)
+
+        @pl.when(z > 0)
+        def _():
+            whole_env(1).wait_recv()
 
         def step(j, carry):
             p = lax.rem(j, 2)
@@ -339,14 +403,16 @@
             @pl.when(j != site)
             def _():
                 remote(bt.at[j], bt.at[j], bt_send, bt_recv.at[j], z * 2).wait_recv()
-                whole_ket(j, over_send).wait_recv()
-
-            all_rows(p).wait_recv()
-            left = jnp.dot(bt[j], env[p], preferred_element_type=F32).astype(BF16)
-            for k in range(TRIP):
-                prod[k] = jnp.dot(
-                    left[k * ROWS:(k + 1) * ROWS], kets[j, k], preferred_element_type=F32
-                )
+
+                @pl.when(j > 1)
+                def _():
+                    whole_ket(j, over_send).wait_recv()
+
+            @pl.when(j > 1)
+            def _():
+                all_rows(p).wait_recv()
+
+            products(bt[j], env[p], j)
             fetch(j, p).wait()
             scatter(p)
 
@@ -354,8 +420,15 @@
             def _():
                 fetch_table(j + 1, 1 - p)
 
-            all_parts(1 - p).wait_send()
-            all_rows(p).wait_send()
+            @pl.when(j > 1)
+            def _():
+                some_parts(1 - p, 0, N_PLANE).wait_send()
+                all_rows(p).wait_send()
+
+            @pl.when((j == 1) & (z == 0))
+            def _():
+                for d in COLUMN:
+                    whole_env(1).wait_send()
 
             @pl.when(j == z * 2)
             def _():
@@ -366,7 +439,7 @@
             def _():
                 out_ref[...] = env[p]
 
-            @pl.when((j == site - 3) & (site < STEPS))
+            @pl.when((j == jnp.maximum(site - 3, 1)) & (site > 1) & (site < STEPS))
             def _():
                 start_bt()
 
@@ -382,7 +455,7 @@
             out_ref[...] = env[last]
 
         all_rows(last).wait_send()
-        all_parts(1 - last).wait_send()
+        some_parts(1 - last, 0, N_PLANE).wait_send()
 
         @pl.when(z > 0)
         def _():
@@ -398,10 +471,21 @@
         def _():
             whole_ket(site, over_send).wait_send()
 
-        @pl.when(site == 1)
+        @pl.when(z < 3)
         def _():
             whole_ket(1, up_send).wait_send()
+
+        @pl.when(z == 3)
+        def _():
+            whole_ket(1, up_send, TRIP // 2).wait_send()
+
+        @pl.when((z == 0) | (z > 5))
+        def _():
             whole_ket(1, down_send).wait_send()
+
+        @pl.when(z == 5)
+        def _():
+            whole_ket(1, down_send, TRIP // 2).wait_send()
 
 
 def run_chain(env, bra, ket, outputs, terms, owner, weight):
@@ -424,14 +508,15 @@
             pltpu.VMEM((TILE, TILE), BF16),
             pltpu.VMEM((NZ, TRIP * ROWS, TILE), BF16),
             pltpu.VMEM((2 * NZ, TRIP * ROWS, TILE), BF16),
-            pltpu.VMEM((NZ, TRIP * ROWS, TILE), BF16),
-            pltpu.VMEM((TRIP * ROWS, TILE), BF16),
+            pltpu.VMEM((NZ, SLOTS, ROWS, TILE), BF16),
+            pltpu.VMEM((NZ, SLOTS, ROWS, TILE), BF16),
             pltpu.VMEM((2 * NZ, TRIP, TILE, TILE), BF16),
             pltpu.VMEM((2 * NZ, 8, TILE), jnp.int32),
             pltpu.SMEM((2, 8, TILE), jnp.int32),
-            dma((2,)), dma((2,)), dma((2,)), dma((2,)), dma, dma, dma, dma((2 * NZ,)),
-            dma, dma, dma, dma((2 * NZ,)), dma((2,)), dma((2,)),
+            dma((2,)), dma((2, 2)), dma((2,)), dma((2,)), dma, dma, dma, dma((2 * NZ,)),
+            dma, dma((NZ,)), dma, dma((2 * NZ,)), dma((2,)), dma((2,)),
             dma, dma, dma, dma((2 * NZ, PIECES)),
+            pltpu.SemaphoreType.REGULAR,
         ],
         compiler_params=pltpu.CompilerParams(
             collective_id=0, has_side_effects=True, vmem_limit_bytes=56 << 20

time: 180 us -> 175 us (0.972)
  Pallas kernels: 178 us -> 173 us
    pallas_call x1, Pallas kernels: 178 us -> 173 us  [run_chain(): pl.pallas_call(chain, out_shape=jax.ShapeDtypeStruct((TILE, TILE), BF16),...]
where the time goes in v4:
time: 175 us
  Pallas kernels  173 us (99%)
    pallas_call x1, Pallas kernels, run_chain(): pl.pallas_call(chain, out_shape=jax.ShapeDtypeStruct((TILE, TILE), BF16),...  173 us

profile of v4, /device:TPU:1, one launch (start us, length us, event | category | flops | bytes accessed | tf_op | source)
XLA Modules:
  0.0 174.7 jit_solution(8935774860348301902)
XLA Ops:
  0.0 173.3 %chain.1 = bf16[128,128]{1,0:T(8,128)(2,1)} custom-call(bf16[128,128]{1,0:T(8,128)(2,1)} %bitcast.10, bf16[16,128,128]{2,1,0:T(8,128)(2,1)} %bitcast.7, bf16[16,128,128]{2,1,0:T(8,128)(2,1)} %bitcast.8, s32[16]{0:T(128)} %bitcast.11, s32[16]{0:T(128)} %bitcast.12, s32[32]{0:T(128)} %owner_ref.1, f32[8]{0:T(128)} %bitcast.13), custom_call_target="tpu_custom_call" | custom-call | tf_op jit(solution)/shard_map/chain/pallas_call | solution.py:496
  173.3 1.4 copy.9

commit v5 on v4

--- a/solution.py
+++ b/solution.py
@@ -98,10 +98,11 @@
 
     def products(bt_chunk, block, j):
         left = jnp.dot(bt_chunk, block, preferred_element_type=F32).astype(BF16)
-        for k in range(TRIP):
-            prod[k] = jnp.dot(
-                left[k * ROWS:(k + 1) * ROWS], kets[j, k], preferred_element_type=F32
-            )
+        for k in range(0, TRIP, 2):
+            pair = jnp.concatenate([kets[j, k], kets[j, k + 1]], axis=1)
+            both = jnp.dot(left[k * ROWS:(k + 2) * ROWS], pair, preferred_element_type=F32)
+            prod[k] = both[:ROWS, :TILE]
+            prod[k + 1] = both[ROWS:, TILE:]
 
     def summed(p, slot):
         return (prod[lookup[p, 0, slot]] + prod[lookup[p, 1, slot]]).astype(BF16)
@@ -439,7 +440,7 @@
             def _():
                 out_ref[...] = env[p]
 
-            @pl.when((j == jnp.maximum(site - 3, 1)) & (site > 1) & (site < STEPS))
+            @pl.when((j == jnp.maximum(site - 2, 1)) & (site > 1) & (site < STEPS))
             def _():
                 start_bt()
 

time: 175 us -> 173 us (0.989)
  Pallas kernels: 173 us -> 171 us
    pallas_call x1, Pallas kernels: 173 us -> 171 us  [run_chain(): pl.pallas_call(chain, out_shape=jax.ShapeDtypeStruct((TILE, TILE), BF16),...]
where the time goes in v5:
time: 173 us; the launch traced here: 172 us
  Pallas kernels  171 us (99%)
    pallas_call x1, Pallas kernels, run_chain(): pl.pallas_call(chain, out_shape=jax.ShapeDtypeStruct((TILE, TILE), BF16),...  171 us

profile of v5, /device:TPU:1, one launch (start us, length us, event | category | flops | bytes accessed | tf_op | source)
XLA Modules:
  0.0 172.3 jit_solution(8525513038663884272)
XLA Ops:
  0.0 170.9 %chain.1 = bf16[128,128]{1,0:T(8,128)(2,1)} custom-call(bf16[128,128]{1,0:T(8,128)(2,1)} %bitcast.10, bf16[16,128,128]{2,1,0:T(8,128)(2,1)} %bitcast.7, bf16[16,128,128]{2,1,0:T(8,128)(2,1)} %bitcast.8, s32[16]{0:T(128)} %bitcast.11, s32[16]{0:T(128)} %bitcast.12, s32[32]{0:T(128)} %owner_ref.1, f32[8]{0:T(128)} %bitcast.13), custom_call_target="tpu_custom_call" | custom-call | tf_op jit(solution)/shard_map/chain/pallas_call | solution.py:497
  170.9 1.4 copy.9

commit v6 on v5

--- a/solution.py
+++ b/solution.py
@@ -20,6 +20,7 @@
 PIECES = 16
 PIECE = TRIP // PIECES
 LEAD = 8
+WIDE = 2
 
 
 def hops(offset):
@@ -156,13 +157,16 @@
             fetch(0, 0).wait()
 
             def chunk(c, carry):
-                products(bt_out[c], env_ref[...], 0)
-                for i in range(SLOTS):
-                    first_out[c, i] = summed(0, sector if i == N_PLANE else slot_at(PLANE[i]))
-                    send_first(c, i).start()
+                for h in range(WIDE):
+                    products(bt_out[c * WIDE + h], env_ref[...], 0)
+                    for i in range(SLOTS):
+                        to = sector if i == N_PLANE else slot_at(PLANE[i])
+                        first_out[c, i, h * ROWS:(h + 1) * ROWS] = summed(0, to)
+                        if h == WIDE - 1:
+                            send_first(c, i).start()
                 return carry
 
-            lax.fori_loop(0, NZ, chunk, 0)
+            lax.fori_loop(0, NZ // WIDE, chunk, 0)
             out_ref[...] = env_ref[...]
 
         @pl.when(z > 0)
@@ -382,14 +386,14 @@
                 total = first_in[c, 0].astype(F32)
                 for i in range(1, SLOTS):
                     total += first_in[c, i].astype(F32)
-                part_rows = pl.ds(pl.multiple_of(c * ROWS, ROWS), ROWS)
+                part_rows = pl.ds(pl.multiple_of(c * (WIDE * ROWS), WIDE * ROWS), WIDE * ROWS)
                 env[1, part_rows] = total.astype(BF16)
                 for d in COLUMN:
                     held = env.at[1, part_rows]
                     remote(held, held, env_send.at[1], env_recv.at[1], plane_at(d) * 2 + 1).start()
                 return carry
 
-            lax.fori_loop(0, NZ, chunk, 0)
+            lax.fori_loop(0, NZ // WIDE, chunk, 0)
 
         def whole_env(q):
             return remote(env.at[q], env.at[q], env_send.at[q], env_recv.at[q], plane_at(1) * 2 + 1)
@@ -509,8 +513,8 @@
             pltpu.VMEM((TILE, TILE), BF16),
             pltpu.VMEM((NZ, TRIP * ROWS, TILE), BF16),
             pltpu.VMEM((2 * NZ, TRIP * ROWS, TILE), BF16),
-            pltpu.VMEM((NZ, SLOTS, ROWS, TILE), BF16),
-            pltpu.VMEM((NZ, SLOTS, ROWS, TILE), BF16),
+            pltpu.VMEM((NZ // WIDE, SLOTS, WIDE * ROWS, TILE), BF16),
+            pltpu.VMEM((NZ // WIDE, SLOTS, WIDE * ROWS, TILE), BF16),
             pltpu.VMEM((2 * NZ, TRIP, TILE, TILE), BF16),
             pltpu.VMEM((2 * NZ, 8, TILE), jnp.int32),
             pltpu.SMEM((2, 8, TILE), jnp.int32),

time: 173 us -> 172 us (level)
  no operation moved by 1% of the time
where the time goes in v6:
time: 172 us
  Pallas kernels  170 us (99%)
    pallas_call x1, Pallas kernels, run_chain(): pl.pallas_call(chain, out_shape=jax.ShapeDtypeStruct((TILE, TILE), BF16),...  170 us

profile of v6, /device:TPU:1, one launch (start us, length us, event | category | flops | bytes accessed | tf_op | source)
XLA Modules:
  0.0 171.8 jit_solution(4875802691513678711)
XLA Ops:
  0.0 170.5 %chain.1 = bf16[128,128]{1,0:T(8,128)(2,1)} custom-call(bf16[128,128]{1,0:T(8,128)(2,1)} %bitcast.10, bf16[16,128,128]{2,1,0:T(8,128)(2,1)} %bitcast.7, bf16[16,128,128]{2,1,0:T(8,128)(2,1)} %bitcast.8, s32[16]{0:T(128)} %bitcast.11, s32[16]{0:T(128)} %bitcast.12, s32[32]{0:T(128)} %owner_ref.1, f32[8]{0:T(128)} %bitcast.13), custom_call_target="tpu_custom_call" | custom-call | tf_op jit(solution)/shard_map/chain/pallas_call | solution.py:501
  170.5 1.4 copy.9

commit v7 on v6

--- a/solution.py
+++ b/solution.py
@@ -140,14 +140,17 @@
     upper = lax.broadcasted_iota(jnp.int32, (8, TILE), 0) == 0
     tables[site] = jnp.where(upper, first, second)
 
-    own_bra.wait()
-    for k in range(TRIP):
-        turned = jnp.transpose(bra[k].astype(F32)) * weight_ref[terms_ref[k]]
-        bt_out[:, k * ROWS:(k + 1) * ROWS, :] = turned.astype(BF16).reshape(NZ, ROWS, TILE)
+    def turn_bras():
+        own_bra.wait()
+        for k in range(TRIP):
+            turned = jnp.transpose(bra[k].astype(F32)) * weight_ref[terms_ref[k]]
+            bt_out[:, k * ROWS:(k + 1) * ROWS, :] = turned.astype(BF16).reshape(NZ, ROWS, TILE)
+
     own_ket.wait()
 
     @pl.when(core == 0)
     def _():
+        turn_bras()
         pl.semaphore_wait(barrier, N_COLUMN + 3 + jnp.where(z == 0, N_PLANE, 0))
 
         @pl.when(z == 0)
@@ -278,7 +281,6 @@
     @pl.when(core == 1)
     def _():
         prod[TRIP] = jnp.zeros((ROWS, TILE), F32)
-        bt[site] = bt_out[z]
         pl.semaphore_wait(barrier, N_PLANE + N_COLUMN + jnp.where(z == 0, 0, 1))
         @pl.when(site < STEPS)
         def _():
@@ -310,6 +312,8 @@
                 ket_piece(1, q, up_send, site).wait_recv()
 
         first_kets(range(PIECES), z == 0, z == 0, source=True)
+        turn_bras()
+        bt[site] = bt_out[z]
 
         @pl.when(site == 1)
         def _():

time: 172 us -> 172 us (level)
  no operation moved by 1% of the time
where the time goes in v7:
time: 172 us
  Pallas kernels  170 us (99%)
    pallas_call x1, Pallas kernels, run_chain(): pl.pallas_call(chain, out_shape=jax.ShapeDtypeStruct((TILE, TILE), BF16),...  170 us

profile of v7, /device:TPU:1, one launch (start us, length us, event | category | flops | bytes accessed | tf_op | source)
XLA Modules:
  0.0 171.8 jit_solution(16736165761841936748)
XLA Ops:
  0.0 170.4 %chain.1 = bf16[128,128]{1,0:T(8,128)(2,1)} custom-call(bf16[128,128]{1,0:T(8,128)(2,1)} %bitcast.10, bf16[16,128,128]{2,1,0:T(8,128)(2,1)} %bitcast.7, bf16[16,128,128]{2,1,0:T(8,128)(2,1)} %bitcast.8, s32[16]{0:T(128)} %bitcast.11, s32[16]{0:T(128)} %bitcast.12, s32[32]{0:T(128)} %owner_ref.1, f32[8]{0:T(128)} %bitcast.13), custom_call_target="tpu_custom_call" | custom-call | tf_op jit(solution)/shard_map/chain/pallas_call | solution.py:505
  170.4 1.4 copy.9
